TPU v7x, 32 devices: a whole 2x2x4 slice. The times are simulated.
32 devices in a mesh: sect: 2 (over y), node: 4 (over z), fn: 2 (over x), sub: 2 (over core).
Axes of the slice: x: 2, y: 2, z: 4, core: 2. Of those that a mesh axis runs over, the one named last changes fastest.
Arguments:
- volume_grad: bfloat16 [2048, 32, 128], P(('sect', 'node', 'fn', 'sub')), parts along dimension 0, may hold values from -0.5 to 0.5
- volume_coords: float32 [2048, 3, 128], P(('sect', 'node', 'fn', 'sub')), parts along dimension 0, may hold values from -2.1366198 to 3
- support: int32 [2048, 32], P(('sect', 'node', 'fn', 'sub')), parts along dimension 0, may hold values from 0 to 31
- control_coords: float32 [64, 3, 128], P(('sect', 'node')), parts along dimension 0, may hold values from -2.1366198 to 3
- neighbours: int32 [64, 4], P(('sect', 'node')), parts along dimension 0, may hold values from 0 to 31
- block_inverse: float32 [64, 128, 128], P(('sect', 'node')), parts along dimension 0, may hold values from -0.09375 to 0.09375
Outputs:
- control_gradient: float32 [64, 32, 128], P(('sect', 'node')), parts along dimension 0
- adjoint: float32 [64, 32, 128], P(('sect', 'node')), parts along dimension 0
There are 2 independent parts, one for each index of `sect`. A program takes and returns all parts, laid end to end along the dimension named above; each array names one. Nothing has to cross between parts.
All inputs are finite; a program needn't handle non-finite values.
Results may differ from a plain program's by a relative error of at most 0.0034.
Values may be sent and summed in bfloat16 or wider, within the bound.
No kernel may reach another device: no remote copies, remote signals or barrier semaphores. Data moves between devices by JAX's collectives and lax.ppermute only.
A program may use at most 64 MiB of HBM per device.

v0:
```python
import jax
import jax.numpy as jnp
from jax import lax
from jax.sharding import PartitionSpec as P

SWEEPS = 2


RADIUS = 1.2


def wendland(points, centers):
    diff = points[..., :, :, None] - centers[..., :, None, :]
    dist = jnp.sqrt(jnp.sum(diff * diff, axis=-3))
    ratio = dist / RADIUS
    inside = jnp.maximum(1.0 - ratio, 0.0)
    return (inside**4 * (4.0 * ratio + 1.0)).astype(jnp.bfloat16)


def local(volume_grad, volume_coords, support, control_coords, neighbours, block_inverse):
    all_centers = lax.all_gather(control_coords, "node", axis=0, tiled=True)
    blocks = volume_grad.shape[0]
    funcs = volume_grad.shape[1]
    width = volume_grad.shape[2]
    listed = support.shape[1]
    group = 2
    count = blocks // group
    grads = volume_grad.reshape(count, group, funcs, width)
    coords = volume_coords.reshape(count, group, 3, width)
    lists = support.reshape(count, group, listed)

    def step(total, items):
        block_grads, block_coords, block_lists = items
        centers = all_centers[block_lists]
        tiles_phi = wendland(block_coords[:, None], centers)
        tiles = jnp.einsum(
            "gfi,gkij->gkfj", block_grads, tiles_phi, preferred_element_type=jnp.float32
        )
        total = total.at[block_lists.reshape(-1)].add(tiles.reshape(-1, funcs, width))
        return (total, None)

    empty = jnp.zeros((all_centers.shape[0], funcs, width), jnp.float32)
    partial_value, _ = lax.scan(step, empty, (grads, coords, lists))
    owned = lax.psum_scatter(partial_value, "node", scatter_dimension=0, tiled=True)
    control_gradient = lax.psum(owned, ("fn", "sub"))
    adjoint = jnp.einsum(
        "cfi,cij->cfj", control_gradient, block_inverse, precision=lax.Precision.HIGHEST
    )
    pair_phi = wendland(all_centers[neighbours], control_coords[:, None])
    for sweep in range(SWEEPS):
        values = lax.all_gather(adjoint.astype(jnp.bfloat16), "node", axis=0, tiled=True)
        near = values[neighbours]
        coupling = jnp.einsum("ckfi,ckij->cfj", near, pair_phi, preferred_element_type=jnp.float32)
        adjoint = jnp.einsum(
            "cfi,cij->cfj",
            control_gradient - coupling,
            block_inverse,
            precision=lax.Precision.HIGHEST,
        )
    return (control_gradient, adjoint)


def solution(mesh):
    return jax.shard_map(
        local,
        mesh=mesh,
        in_specs=(
            P(("sect", "node", "fn", "sub"), None, None),
            P(("sect", "node", "fn", "sub"), None, None),
            P(("sect", "node", "fn", "sub"), None),
            P(("sect", "node"), None, None),
            P(("sect", "node"), None),
            P(("sect", "node"), None, None),
        ),
        out_specs=(P(("sect", "node"), None, None), P(("sect", "node"), None, None)),
        check_vma=False,
    )
```

profile of v0, /device:TPU:0, one launch (start us, length us, event | category | flops | bytes accessed | tf_op | source)
XLA Modules:
  0.0 401.6 jit_solution(12092101449089686073)
XLA Ops:
  9.0 15.0 %all_gather.9 = f32[32,3,128]{2,0,1:T(8,128)S(1)} all-gather(f32[8,3,128]{2,0,1:T(8,128)} %param.11), channel_id=1, replica_groups=mesh['sect'=2,'node'=4,'fn'=2,'sub'=2] {'node'}, dimensions={0}, use_global_device_ids=true | all-gather | bytes 61440 | tf_op jit(solution)/shard_map/all_gather | solution.py:21
  24.1 280.2 %while.12 = (s32[]{:T(128)}, f32[32,32,128]{2,1,0:T(8,128)S(1)}, s32[32,2,32]{2,1,0:T(2,128)S(1)}, f32[32,2,3,128]{3,2,1,0:T(4,128)S(1)}, f32[32,3,128]{2,1,0:T(...) while((s32[]{:T(128)}, f32[32,32,128]{2,1,0:T(8,128)S(1)}, s32[32,2,32]{2,1,0:T(2,128)S(1)}, ...), condition=%wide.region_3.4_spmd, body=%wide.region_0.3_spmd.sunk | while | flops 85198208 | bytes 12910689 | solution.py:43
  29.7 3.1 scatter_fusion
  38.5 3.1 scatter_fusion
  44.2 3.0 fusion.27
  47.2 3.1 scatter_fusion
  53.0 3.0 fusion.27
  56.0 3.1 scatter_fusion
  61.7 3.0 fusion.27
  64.8 3.1 scatter_fusion
  73.5 3.1 scatter_fusion
  82.3 3.1 scatter_fusion
  88.0 3.0 fusion.27
  91.0 3.1 scatter_fusion
  99.8 3.1 scatter_fusion
  108.5 3.1 scatter_fusion
  117.3 3.1 scatter_fusion
  126.0 3.1 scatter_fusion
  134.8 3.1 scatter_fusion
  140.5 3.0 fusion.27
  143.6 3.1 scatter_fusion
  149.3 3.0 fusion.27
  152.3 3.1 scatter_fusion
  161.1 3.1 scatter_fusion
  169.8 3.1 scatter_fusion
  178.6 3.1 scatter_fusion
  184.3 3.0 fusion.27
  187.3 3.1 scatter_fusion
  196.1 3.1 scatter_fusion
  204.8 3.1 scatter_fusion
  213.6 3.1 scatter_fusion
  219.3 3.0 fusion.27
  222.4 3.1 scatter_fusion
  231.1 3.1 scatter_fusion
  239.9 3.1 scatter_fusion
  248.6 3.1 scatter_fusion
  257.4 3.1 scatter_fusion
  263.1 3.0 fusion.27
  266.1 3.1 scatter_fusion
  274.9 3.1 scatter_fusion
  283.7 3.1 scatter_fusion
  292.4 3.1 scatter_fusion
  301.2 3.1 scatter_fusion
  306.0 3.4 multiply_reduce_fusion.1
  309.4 18.7 %reduce-scatter.2.cloned.1.call-done = f32[8,32,128]{2,1,0:T(8,128)} async-done(((f32[32,32,128]{2,1,0:T(8,128)}), f32[8,32,128]{2,1,0:T(8,128)}) %reduce-scatter.2.cloned.1.call-update) | async-done | bytes 131088 | tf_op jit(solution)/shard_map/reduce_scatter | solution.py:44
  330.8 29.3 %all-reduce.2.cloned.1.call-done = f32[8,32,128]{2,1,0:T(8,128)} async-done(((f32[8,32,128]{2,1,0:T(8,128)}), f32[8,32,128]{2,1,0:T(8,128)}) %all-reduce.2.cloned.1.call-update) | async-done | bytes 131088 | tf_op jit(solution)/shard_map/psum | solution.py:45
  361.6 13.9 %all_gather.10 = bf16[32,32,128]{2,1,0:T(8,128)(2,1)S(1)} all-gather(bf16[8,32,128]{2,1,0:T(8,128)(2,1)S(1)} %convolution_convert_fusion.1), channel_id=1, replica_groups=mesh['sect'=2,'node'=4,'fn'=2,'sub'=2] {'node'}, dimensions={0}, use_global_device_ids=true | all-gather | bytes 327680 | tf_op jit(solution)/shard_map/all_gather | solution.py:51
  377.8 14.1 %all_gather.11 = bf16[32,32,128]{2,1,0:T(8,128)(2,1)S(1)} all-gather(bf16[8,32,128]{2,1,0:T(8,128)(2,1)S(1)} %convolution_convert_fusion), channel_id=1, replica_groups=mesh['sect'=2,'node'=4,'fn'=2,'sub'=2] {'node'}, dimensions={0}, use_global_device_ids=true | all-gather | bytes 327680 | tf_op jit(solution)/shard_map/all_gather | solution.py:51
  (312 shorter events, 164.1 us)
Async XLA Ops:
  7.2 352.9 %copy-start = (f32[8,128,128]{2,1,0:T(8,128)S(1)}, f32[8,128,128]{2,1,0:T(8,128)}, u32[]{:S(2)}) copy-start(f32[8,128,128]{2,1,0:T(8,128)} %param.13) | copy-start | bytes 1572868
  7.2 320.9 %reduce-scatter.2.cloned.1.call-start = ((), (), s32[]{:S(2)}) async-start(), calls=%async_computation.1 | async-start | bytes 655360 | tf_op jit(solution)/shard_map/reduce_scatter | solution.py:44
  24.1 281.1 %copy-start.3 = (f32[8,3,128]{2,0,1:T(8,128)S(1)}, f32[8,3,128]{2,0,1:T(8,128)}, u32[]{:S(2)}) copy-start(f32[8,3,128]{2,0,1:T(8,128)} %param.11) | copy-start | bytes 36868
  24.1 281.1 %copy-start.4 = (s32[8,4]{0,1:T(4,128)S(1)}, s32[8,4]{0,1:T(4,128)}, u32[]{:S(2)}) copy-start(s32[8,4]{0,1:T(4,128)} %param.12) | copy-start | bytes 388
  304.3 0.8 copy-start.1
  305.1 55.0 %all-reduce.2.cloned.1.call-start = ((), (), s32[]{:S(2)}) async-start(), calls=%async_computation.2 | async-start | bytes 262144 | tf_op jit(solution)/shard_map/psum | solution.py:45
  360.1 32.5 %copy-start.2 = (f32[8,32,128]{2,1,0:T(8,128)S(1)}, f32[8,32,128]{2,1,0:T(8,128)}, u32[]{:S(2)}) copy-start(f32[8,32,128]{2,1,0:T(8,128)} %all-reduce.2.cloned.1.call-done) | copy-start | bytes 393220
Sparse Core Ops, SparseCore 0:
  305.3 22.8 reduce-scatter.1
  330.4 29.6 all-reduce.1
where the time goes:
time: 405 us; the launch traced here: 402 us
  other arithmetic  161 us (40%)
  matrix products  102 us (25%)
  waiting for transfers between devices  48 us (12%)
  blocking collectives  43 us (11%)
  local copies, waits for them, and re-layouts  31.8 us (8%)
  between operations  14.2 us (4%)
    scatter-add x32, other arithmetic, step(): total.at[block_lists.reshape(-1)].add(tiles.reshape(-1, funcs, width))  100 us
    dot_general x32, matrix products, step(): jnp.einsum('gfi,gkij->gkfj', block_grads, tiles_phi, preferred_element_ty...  97 us
    reduce_sum x33, other arithmetic, wendland(): dist = jnp.sqrt(jnp.sum(diff * diff, axis=-3))  57.5 us
    psum x1, waiting for transfers between devices, local(): control_gradient = lax.psum(owned, ('fn', 'sub'))  29.3 us
    all_gather x2, blocking collectives, local(): lax.all_gather(adjoint.astype(jnp.bfloat16), 'node', axis=0, tiled=True)  28 us
    gather x32, local copies, waits for them, and re-layouts, step(): centers = all_centers[block_lists]  21 us
    reduce_scatter x1, waiting for transfers between devices, local(): lax.psum_scatter(partial_value, 'node', scatter_dimension=0, tiled=True)  18.7 us
    all_gather x1, blocking collectives, local(): all_centers = lax.all_gather(control_coords, 'node', axis=0, tiled=True)  15 us
  transfers between devices with their start and end apart: 2, of which 2 were waited for; matrix products, arithmetic and copies ran while one was open for 2% of the time, Pallas kernels for 0%

commit v1 on v0

v1 whole, which is shorter than its diff:
```python
import functools

import jax
import jax.numpy as jnp
from jax import lax
from jax.experimental import pallas as pl
from jax.experimental.pallas import tpu as pltpu
from jax.sharding import PartitionSpec as P

SWEEPS = 2
RADIUS = 1.2
C = 4.0**0.2
GEO = 64
CHUNKS = 4
f32, bf16 = jnp.float32, jnp.bfloat16


def params():
    return pltpu.CompilerParams(vmem_limit_bytes=56 << 20)


def phi_of(square):
    root = jnp.maximum(square, 1e-12)
    root = root * lax.rsqrt(root)
    inside = jnp.maximum(C - root, 0.0)
    twice = inside * inside
    return ((twice * twice) * (1.25 * C - inside)).astype(bf16)


def split3(v):
    a = v.astype(bf16).astype(f32)
    b = (v - a).astype(bf16).astype(f32)
    return (a, b, v - a - b)


def coords_of(ref):
    scale = C / RADIUS
    return [ref[:, d, :] * scale for d in range(3)]


def left_rows(ref):
    xyz = coords_of(ref)
    rows = []
    for v in xyz:
        parts = split3(v)
        rows += [parts[a] for a in range(3) for b in range(3)]
    rows += list(split3(sum(v * v for v in xyz)))
    return rows + [jnp.ones_like(xyz[0])] * 3


def right_rows(ref):
    xyz = coords_of(ref)
    rows = []
    for v in xyz:
        parts = split3(v)
        rows += [-2.0 * parts[b] for a in range(3) for b in range(3)]
    rows += [jnp.ones_like(xyz[0])] * 3
    return rows + list(split3(sum(v * v for v in xyz)))


def fill_rows(scratch, rows):
    scratch[...] = jnp.zeros_like(scratch)
    for g, row in enumerate(rows):
        scratch[:, g, :] = row


def shell_features_kernel(coords_ref, out_ref, scratch):
    fill_rows(scratch, left_rows(coords_ref))
    blocks = coords_ref.shape[0]
    head = out_ref.shape[2] - GEO

    def one(s, _):
        lane = lax.broadcasted_iota(jnp.int32, (128, head), 1)
        out_ref[s, :, 0:head] = jnp.where(lane == s, 1.0, 0.0).astype(bf16)
        out_ref[s, :, head:] = scratch[s].T.astype(bf16)
        return 0

    lax.fori_loop(0, blocks, one, 0)


def control_features_kernel(coords_ref, left_ref, right_ref, scratch):
    fill_rows(scratch, left_rows(coords_ref))
    blocks = coords_ref.shape[0]

    def one(c, _):
        left_ref[c] = scratch[c].T.astype(bf16)
        return 0

    lax.fori_loop(0, blocks, one, 0)
    fill_rows(scratch, right_rows(coords_ref))
    right_ref[...] = scratch[...].astype(bf16)


def chunk_kernel(
    chunk, per, tile, side_ref, left_ref, right_ref, grad_ref, support_ref, keep_ref, send_ref,
    rhs, total, d0, d1, p0, p1,
):
    blocks = grad_ref.shape[0]
    head = rhs.shape[1] - GEO
    steps = blocks // tile
    pairs = per // 2
    whole = pairs * steps
    counts = []
    listed = support_ref[...]
    for c in range(per):
        hit = jnp.where(listed == chunk * per + c, 1, 0)
        counts.append(jnp.sum(hit, axis=1, keepdims=True))
    most = counts[0]
    for c in range(1, per):
        most = jnp.maximum(most, counts[c])
    most = jnp.max(most)
    layers = jnp.int32(0)
    for b in range(support_ref.shape[1].bit_length()):
        layers = layers + jnp.where(most >= (1 << b), 1, 0)
    total[...] = jnp.zeros_like(total)
    for j in range(pairs):
        for q in range(2):
            rhs[j, head:, q * 128 : (q + 1) * 128] = right_ref[2 * j + q]

    def distances(t, d):
        j, i = t // steps, t % steps
        left = left_ref[pl.ds(i * tile, tile)].reshape(tile * 128, head + GEO)
        d[...] = jnp.dot(left, rhs[j], preferred_element_type=f32)

    def values(d, p):
        p[...] = phi_of(d[...])

    def products(t, p, weight):
        j, i = t // steps, t % steps
        g = jnp.concatenate([grad_ref[i * tile + q] for q in range(tile)], axis=1)
        total[j] += weight * jnp.dot(g, p[...], preferred_element_type=f32)

    def layer(b, weight):
        for c in range(per):
            bit = jnp.bitwise_and(lax.shift_right_logical(counts[c], b), 1)
            far = jnp.where(jnp.broadcast_to(bit, (blocks, 128)) == 1, 0.0, 16384.0)
            if head > blocks:
                far = jnp.concatenate([far, jnp.zeros((head - blocks, 128), f32)], axis=0)
            rhs[c // 2, 0:head, (c % 2) * 128 : (c % 2 + 1) * 128] = far.astype(bf16)
        p1[...] = jnp.zeros_like(p1)
        distances(0, d0)

        def two(h, _):
            t = 2 * h
            distances(t + 1, d1)
            values(d0, p0)
            products(jnp.maximum(t - 1, 0), p1, weight)
            distances(jnp.minimum(t + 2, whole - 1), d0)
            values(d1, p1)
            products(t, p0, weight)
            return 0

        lax.fori_loop(0, whole // 2, two, 0)
        products(whole - 1, p1, weight)
        return weight * 2.0

    lax.fori_loop(0, layers, layer, jnp.float32(1.0))
    side = side_ref[0]
    half = per // 2
    for c in range(half):
        for q in range(2):
            pass
    quarter = pairs // 2
    for j in range(quarter):
        mine = total[side * quarter + j]
        other = total[(1 - side) * quarter + j]
        for q in range(2):
            keep_ref[2 * j + q] = mine[:, q * 128 : (q + 1) * 128]
            send_ref[2 * j + q] = other[:, q * 128 : (q + 1) * 128]


def pairs_kernel(near_ref, left_ref, right_ref, inverse_ref, phi_ref, parts_ref):
    blocks, coupled = near_ref.shape

    def one(c, _):
        for k in range(coupled):
            d = jnp.dot(left_ref[near_ref[c, k]], right_ref[c], preferred_element_type=f32)
            phi_ref[c, k * 128 : (k + 1) * 128, :] = phi_of(d)
        inv = inverse_ref[c]
        high = inv.astype(bf16)
        parts_ref[c, 0:128, :] = high
        parts_ref[c, 128:256, :] = (inv - high.astype(f32)).astype(bf16)
        return 0

    lax.fori_loop(0, blocks, one, 0, unroll=2)


def solve_kernel(
    count, me_ref, near_ref, *refs
):
    halves = refs[: 2 * count]
    phi_ref, parts_ref, grad_out, adjoint_out, grads, values0, values1 = refs[2 * count :]
    blocks, coupled = near_ref.shape
    own = grad_out.shape[0]
    half = halves[0].shape[0]
    for h in range(2 * count):
        grads[h * half : (h + 1) * half] = halves[h][...]
    first = me_ref[0] * own

    def through(x, c):
        high = x.astype(bf16)
        low = (x - high.astype(f32)).astype(bf16)
        both = jnp.concatenate(
            [jnp.concatenate([high, high], axis=1), jnp.concatenate([low, jnp.zeros_like(low)], axis=1)],
            axis=0,
        )
        out = jnp.dot(both, parts_ref[c], preferred_element_type=f32)
        rows = x.shape[0]
        return out[:rows] + out[rows:]

    def start(c, _):
        values0[c] = through(grads[c], c).astype(bf16)
        return 0

    lax.fori_loop(0, blocks, start, 0, unroll=4)

    def swept(old, c):
        near = jnp.concatenate([old[near_ref[c, k]] for k in range(coupled)], axis=1)
        coupling = jnp.dot(near, phi_ref[c], preferred_element_type=f32)
        return through(grads[c] - coupling, c)

    old, new = values0, values1
    for sweep in range(SWEEPS - 1):
        def one(c, _, old=old, new=new):
            new[c] = swept(old, c).astype(bf16)
            return 0

        lax.fori_loop(0, blocks, one, 0, unroll=4)
        old, new = new, old

    def last(c, _):
        grad_out[c] = grads[first + c]
        adjoint_out[c] = swept(old, first + c)
        return 0

    lax.fori_loop(0, own, last, 0, unroll=4)


def exchange(x, axis, size, step):
    return lax.ppermute(x, axis, [(i, i ^ step) for i in range(size)])


def gather(x, axis, size):
    me = lax.axis_index(axis)
    out = jnp.zeros((size,) + x.shape, x.dtype)
    out = lax.dynamic_update_index_in_dim(out, x, me, 0)
    for step in range(1, size):
        out = lax.dynamic_update_index_in_dim(out, exchange(x, axis, size, step), me ^ step, 0)
    return out.reshape((size * x.shape[0],) + x.shape[1:])


def add_over(x, axis, size):
    step = 1
    while step < size:
        x = x + exchange(x, axis, size, step)
        step *= 2
    return x


def local(sizes, volume_grad, volume_coords, support, control_coords, neighbours, block_inverse):
    nodes, fns, subs = sizes["node"], sizes["fn"], sizes["sub"]
    blocks, funcs, width = volume_grad.shape
    side = lax.axis_index("sub").astype(jnp.int32).reshape(1)
    me = lax.axis_index("node").astype(jnp.int32).reshape(1)
    all_coords = gather(control_coords, "node", nodes)
    controls = all_coords.shape[0]
    head = -(-(blocks + GEO) // 128) * 128 - GEO

    left = pl.pallas_call(
        shell_features_kernel,
        out_shape=jax.ShapeDtypeStruct((blocks, width, head + GEO), bf16),
        scratch_shapes=[pltpu.VMEM((blocks, GEO, width), f32)],
        compiler_params=params(),
        name="shell_features",
    )(volume_coords)
    control_left, control_right = pl.pallas_call(
        control_features_kernel,
        out_shape=(
            jax.ShapeDtypeStruct((controls, width, GEO), bf16),
            jax.ShapeDtypeStruct((controls, GEO, width), bf16),
        ),
        scratch_shapes=[pltpu.VMEM((controls, GEO, width), f32)],
        compiler_params=params(),
        name="control_features",
    )(all_coords)

    all_near = gather(neighbours, "node", nodes)
    all_inverse = gather(block_inverse, "node", nodes)

    per = controls // CHUNKS
    half = per // 2
    tile = 4
    vmem = pl.BlockSpec(memory_space=pltpu.VMEM)
    smem = pl.BlockSpec(memory_space=pltpu.SMEM)
    halves = []
    for chunk in range(CHUNKS):
        entries = blocks * per * width * width
        keep, send = pl.pallas_call(
            functools.partial(chunk_kernel, chunk, per, tile),
            out_shape=[jax.ShapeDtypeStruct((half, funcs, width), f32)] * 2,
            in_specs=[smem, vmem, vmem, vmem, vmem],
            out_specs=[vmem, vmem],
            scratch_shapes=[
                pltpu.VMEM((per // 2, head + GEO, 2 * width), bf16),
                pltpu.VMEM((per // 2, funcs, 2 * width), f32),
                pltpu.VMEM((tile * width, 2 * width), f32),
                pltpu.VMEM((tile * width, 2 * width), f32),
                pltpu.VMEM((tile * width, 2 * width), bf16),
                pltpu.VMEM((tile * width, 2 * width), bf16),
            ],
            compiler_params=params(),
            cost_estimate=pl.CostEstimate(
                flops=entries * 400, bytes_accessed=4 << 20, transcendentals=entries
            ),
            name=f"chunk_{chunk}",
        )(side, left, control_right[chunk * per : (chunk + 1) * per], volume_grad, support)
        part = keep + exchange(send, "sub", subs, 1)
        part = add_over(part, "fn", fns)
        part = add_over(part, "node", nodes)
        other = exchange(part, "sub", subs, 1)
        halves.append(jnp.where(side[0] == 0, part, other))
        halves.append(jnp.where(side[0] == 0, other, part))

    coupled = neighbours.shape[1]
    phi, parts = pl.pallas_call(
        pairs_kernel,
        out_shape=[
            jax.ShapeDtypeStruct((controls, coupled * width, width), bf16),
            jax.ShapeDtypeStruct((controls, 2 * width, width), bf16),
        ],
        in_specs=[smem, vmem, vmem, vmem],
        out_specs=[vmem, vmem],
        compiler_params=params(),
        name="pairs",
    )(all_near, control_left, control_right, all_inverse)

    own = control_coords.shape[0]
    return tuple(
        pl.pallas_call(
            functools.partial(solve_kernel, CHUNKS),
            out_shape=[jax.ShapeDtypeStruct((own, funcs, width), f32)] * 2,
            in_specs=[smem, smem] + [vmem] * (2 * CHUNKS + 2),
            out_specs=[vmem, vmem],
            scratch_shapes=[
                pltpu.VMEM((controls, funcs, width), f32),
                pltpu.VMEM((controls, funcs, width), bf16),
                pltpu.VMEM((controls, funcs, width), bf16),
            ],
            compiler_params=params(),
            name="solve",
        )(me, all_near, *halves, phi, parts)
    )


def solution(mesh):
    return jax.shard_map(
        functools.partial(local, dict(mesh.shape)),
        mesh=mesh,
        in_specs=(
            P(("sect", "node", "fn", "sub"), None, None),
            P(("sect", "node", "fn", "sub"), None, None),
            P(("sect", "node", "fn", "sub"), None),
            P(("sect", "node"), None, None),
            P(("sect", "node"), None),
            P(("sect", "node"), None, None),
        ),
        out_specs=(P(("sect", "node"), None, None), P(("sect", "node"), None, None)),
        check_vma=False,
    )
```

time: 405 us -> 198 us (0.49)
  the two profiles are of different devices: /device:TPU:0 before, /device:TPU:8 now
where the time goes in v1:
time: 198 us
  Pallas kernels  107 us (54%)
  waiting for transfers between devices  44.3 us (22%)
  starting transfers between devices  31.7 us (16%)
  local copies, waits for them, and re-layouts  8.24 us (4%)
  other arithmetic  5.36 us (3%)
    pallas_call x4, Pallas kernels, local(): pl.pallas_call(functools.partial(chunk_kernel, chunk, per, tile), out_sha...  65.3 us
    ppermute x29, waiting for transfers between devices, exchange(): return lax.ppermute(x, axis, [(i, i ^ step) for i in range(size)])  44.3 us
    ppermute x29, starting transfers between devices, exchange(): return lax.ppermute(x, axis, [(i, i ^ step) for i in range(size)])  31.7 us
    pallas_call x1, Pallas kernels, local(): pl.pallas_call(shell_features_kernel, out_shape=jax.ShapeDtypeStruct((blo...  14.2 us
    pallas_call x1, Pallas kernels, local(): pl.pallas_call(functools.partial(solve_kernel, CHUNKS), out_shape=[jax.Sh...  12.2 us
    pallas_call x1, Pallas kernels, local(): pl.pallas_call(pairs_kernel, out_shape=[jax.ShapeDtypeStruct((controls, c...  9.58 us
    pallas_call x1, Pallas kernels, local(): pl.pallas_call(control_features_kernel, out_shape=(jax.ShapeDtypeStruct((...  5.94 us
    unnamed x18, local copies, waits for them, and re-layouts  4.35 us
  transfers between devices with their start and end apart: 29, of which 8 were waited for; matrix products, arithmetic and copies ran while one was open for 5% of the time, Pallas kernels for 32%

profile of v1, /device:TPU:8, one launch (start us, length us, event | category | flops | bytes accessed | tf_op | source)
XLA Modules:
  0.0 197.8 jit_solution(15925854095457026294)
XLA Ops:
  0.7 3.0 %collective-permute-start.4 = (f32[8,3,128]{2,0,1:T(8,128)}, f32[8,3,128]{2,0,1:T(8,128)S(1)}, u32[]{:S(2)}, u32[]{:S(2)}) collective-permute-start(f32[8,3,128]{2,0,1:T(8,128)} %param.9), channel_id=1, source_target_pairs={{0,8},{4,12},{8,0},{12,4},{1,9},{5,13},{9,1},{13,5},{2,10},{6,14},... | collective-permute-start | bytes 36872 | tf_op jit(solution)/shard_map/ppermute | solution.py:240
  3.7 0.5 collective-permute-start.5
  4.2 0.7 copy_dynamic-update-slice_fusion.3
  5.0 1.6 copy.12.coords_ref
  6.6 14.2 %shell_features.1.left_ref = bf16[64,128,128]{2,1,0:T(8,128)(2,1)} custom-call(f32[64,3,128]{2,1,0:T(4,128)} %copy.12.coords_ref), custom_call_target="tpu_custom_call" | custom-call | tf_op jit(solution)/shard_map/shell_features/pallas_call | solution.py:269
  20.8 0.7 copy.17.support_ref
  21.6 0.6 copy-done.2
  22.2 5.9 %control_features.1 = (bf16[32,128,64]{2,1,0:T(8,128)(2,1)}, bf16[32,64,128]{2,1,0:T(8,128)(2,1)}) custom-call(f32[32,3,128]{2,1,0:T(4,128)} %bitcast.30), custom_call_target="tpu_custom_call" | custom-call | tf_op jit(solution)/shard_map/control_features/pallas_call | solution.py:276
  28.1 1.9 fusion
  30.0 16.3 %chunk_3.1 = (f32[4,32,128]{2,1,0:T(8,128)}, f32[4,32,128]{2,1,0:T(8,128)}) custom-call(s32[1]{0:T(128)} %bitcast.10.side_ref, bf16[64,128,128]{2,1,0:T(8,128)(2,1)} %shell_features.1.left_ref, bf16[8,64,128]{2,1,0:T(8,128)(2,1)} %get-tuple-element.26.right_ref, bf16[64,32,128]{2,1,0:T(8,128)(2,1)} %grad_ref.7, s32[64,32]{1,0:T(8,128)} %copy.17.support_ref), custom_call_target="tpu_custom_call" | custom-call | flops 3355443200 | bytes 4194304 | tf_op jit(solution)/shard_map/chunk_3/pallas_call | solution.py:298
  46.3 16.3 %chunk_2.1 = (f32[4,32,128]{2,1,0:T(8,128)}, f32[4,32,128]{2,1,0:T(8,128)}) custom-call(s32[1]{0:T(128)} %bitcast.10.side_ref, bf16[64,128,128]{2,1,0:T(8,128)(2,1)} %shell_features.1.left_ref, bf16[8,64,128]{2,1,0:T(8,128)(2,1)} %get-tuple-element.27.right_ref, bf16[64,32,128]{2,1,0:T(8,128)(2,1)} %grad_ref.7, s32[64,32]{1,0:T(8,128)} %copy.17.support_ref), custom_call_target="tpu_custom_call" | custom-call | flops 3355443200 | bytes 4194304 | tf_op jit(solution)/shard_map/chunk_2/pallas_call | solution.py:298
  62.6 0.5 collective-permute-start.16
  63.1 16.3 %chunk_1.1 = (f32[4,32,128]{2,1,0:T(8,128)}, f32[4,32,128]{2,1,0:T(8,128)}) custom-call(s32[1]{0:T(128)} %bitcast.10.side_ref, bf16[64,128,128]{2,1,0:T(8,128)(2,1)} %shell_features.1.left_ref, bf16[8,64,128]{2,1,0:T(8,128)(2,1)} %get-tuple-element.28.right_ref, bf16[64,32,128]{2,1,0:T(8,128)(2,1)} %grad_ref.7, s32[64,32]{1,0:T(8,128)} %copy.17.support_ref), custom_call_target="tpu_custom_call" | custom-call | flops 3355443200 | bytes 4194304 | tf_op jit(solution)/shard_map/chunk_1/pallas_call | solution.py:298
  79.5 16.3 %chunk_0.1 = (f32[4,32,128]{2,1,0:T(8,128)}, f32[4,32,128]{2,1,0:T(8,128)}) custom-call(s32[1]{0:T(128)} %bitcast.10.side_ref, bf16[64,128,128]{2,1,0:T(8,128)(2,1)} %shell_features.1.left_ref, bf16[8,64,128]{2,1,0:T(8,128)(2,1)} %get-tuple-element.29.right_ref, bf16[64,32,128]{2,1,0:T(8,128)(2,1)} %grad_ref.7, s32[64,32]{1,0:T(8,128)} %copy.17.support_ref), custom_call_target="tpu_custom_call" | custom-call | flops 3355443200 | bytes 4194304 | tf_op jit(solution)/shard_map/chunk_0/pallas_call | solution.py:298
  95.8 0.5 collective-permute-start.6
  96.3 1.6 collective-permute-start.22
  97.9 0.6 collective-permute-start.17
  98.5 1.6 collective-permute-start.12
  100.1 0.8 add.75
  101.0 0.6 collective-permute-start.7
  101.6 1.2 collective-permute-start.23
  102.8 1.2 collective-permute-start.18
  104.1 1.0 collective-permute-start.13
  105.3 1.4 collective-permute-start.8
  106.7 3.3 %collective-permute-start.24 = (f32[4,32,128]{2,1,0:T(8,128)S(1)}, f32[4,32,128]{2,1,0:T(8,128)S(1)}, u32[]{:S(2)}, u32[]{:S(2)}) collective-permute-start(f32[4,32,128]{2,1,0:T(8,128)S(1)} %add.89), channel_id=1, source_target_pairs={{0,8},{4,12},{8,0},{12,4},{1,9},{5,13},{9,1},{13,5},{2,10},{6,14},... | collective-permute-start | bytes 196616 | tf_op jit(solution)/shard_map/ppermute | solution.py:240
  110.0 0.9 collective-permute-start
  111.2 2.9 %collective-permute-start.14 = (f32[4,32,128]{2,1,0:T(8,128)S(1)}, f32[4,32,128]{2,1,0:T(8,128)S(1)}, u32[]{:S(2)}, u32[]{:S(2)}) collective-permute-start(f32[4,32,128]{2,1,0:T(8,128)S(1)} %add.81), channel_id=1, source_target_pairs={{0,8},{4,12},{8,0},{12,4},{1,9},{5,13},{9,1},{13,5},{2,10},{6,14},... | collective-permute-start | bytes 196616 | tf_op jit(solution)/shard_map/ppermute | solution.py:240
  114.3 1.0 collective-permute-done.24
  115.7 3.4 %collective-permute-start.1 = (s32[8,4]{0,1:T(4,128)S(1)}, s32[8,4]{0,1:T(4,128)S(1)}, u32[]{:S(2)}, u32[]{:S(2)}) collective-permute-start(s32[8,4]{0,1:T(4,128)S(1)} %copy-done.7), channel_id=1, source_target_pairs={{0,8},{4,12},{8,0},{12,4},{1,9},{5,13},{9,1},{13,5},{2,10},{6,14},... | collective-permute-start | bytes 392 | tf_op jit(solution)/shard_map/ppermute | solution.py:240
  119.2 1.5 collective-permute-done.1
  120.7 1.0 collective-permute-start.2
  121.7 2.6 %collective-permute-done.2 = s32[8,4]{0,1:T(4,128)S(1)} collective-permute-done((s32[8,4]{0,1:T(4,128)S(1)}, s32[8,4]{0,1:T(4,128)S(1)}, u32[]{:S(2)}, u32[]{:S(2)}) %collective-permute-start.2) | collective-permute-done | bytes 160 | tf_op jit(solution)/shard_map/ppermute | solution.py:240
  124.3 3.8 %collective-permute-start.26 = (f32[8,128,128]{2,1,0:T(8,128)S(1)}, f32[8,128,128]{2,1,0:T(8,128)S(1)}, u32[]{:S(2)}, u32[]{:S(2)}) collective-permute-start(f32[8,128,128]{2,1,0:T(8,128)S(1)} %copy-done.1), channel_id=1, source_target_pairs={{0,4},{4,0},{8,12},{12,8},{1,5},{5,1},{9,13},{13,9},{2,6},{6,2},{1... | collective-permute-start | bytes 1572872 | tf_op jit(solution)/shard_map/ppermute | solution.py:240
  128.1 0.7 copy.23
  128.8 1.0 collective-permute-start.27
  129.8 0.6 collective-permute-start.28
  130.5 0.9 add.78
  131.4 0.6 collective-permute-start.15
  132.0 1.5 broadcast_select_fusion
  133.5 0.7 broadcast_select_fusion.2
  134.2 0.7 broadcast_select_fusion.4
  134.8 0.7 broadcast_select_fusion.6
  135.5 11.1 %collective-permute-done.26 = f32[8,128,128]{2,1,0:T(8,128)S(1)} collective-permute-done((f32[8,128,128]{2,1,0:T(8,128)S(1)}, f32[8,128,128]{2,1,0:T(8,128)S(1)}, u32[]{:S(2)}, u32[]{:S(2)}) %collective-permute-start.26) | collective-permute-done | bytes 524320 | tf_op jit(solution)/shard_map/ppermute | solution.py:240
  146.7 18.0 %collective-permute-done.27 = f32[8,128,128]{2,1,0:T(8,128)S(1)} collective-permute-done((f32[8,128,128]{2,1,0:T(8,128)S(1)}, f32[8,128,128]{2,1,0:T(8,128)S(1)}, u32[]{:S(2)}, u32[]{:S(2)}) %collective-permute-start.27) | collective-permute-done | bytes 524320 | tf_op jit(solution)/shard_map/ppermute | solution.py:240
  164.7 9.8 %collective-permute-done.28 = f32[8,128,128]{2,1,0:T(8,128)S(1)} collective-permute-done((f32[8,128,128]{2,1,0:T(8,128)S(1)}, f32[8,128,128]{2,1,0:T(8,128)S(1)}, u32[]{:S(2)}, u32[]{:S(2)}) %collective-permute-start.28) | collective-permute-done | bytes 524320 | tf_op jit(solution)/shard_map/ppermute | solution.py:240
  174.5 1.4 copy-done
  175.9 9.6 %pairs.1 = (bf16[32,512,128]{2,1,0:T(8,128)(2,1)}, bf16[32,256,128]{2,1,0:T(8,128)(2,1)}) custom-call(s32[32,4]{1,0:T(8,128)} %bitcast.31, bf16[32,128,64]{2,1,0:T(8,128)(2,1)} %get-tuple-element.23.left_ref, bf16[32,64,128]{2,1,0:T(8,128)(2,1)} %get-tuple-element.14.right_ref, f32[32,128,128]{2,1,0:T(8,128)} %bitcast.29), custom_call_target="tpu_custom_call" | custom-call | tf_op jit(solution)/shard_map/pairs/pallas_call | solution.py:325
  185.5 12.2 %solve.1 = (f32[8,32,128]{2,1,0:T(8,128)}, f32[8,32,128]{2,1,0:T(8,128)}) custom-call(s32[1]{0:T(128)} %bitcast.me_ref, s32[32,4]{1,0:T(8,128)} %bitcast.32, f32[4,32,128]{2,1,0:T(8,128)} %get-tuple-element.37.refs_0_, f32[4,32,128]{2,1,0:T(8,128)} %get-tuple-element.36.refs_1_, f32[4,32,128]{2,1,0:T(8,128)} %get-tuple-element.35.refs_2_, ...), custom_call_target="tpu_custom_call" | custom-call | tf_op jit(solution)/shard_map/solve/pallas_call | solution.py:339
  (73 shorter events, 1.7 us)
Async XLA Ops:
  0.6 20.2 %copy-start.6 = (s32[64,32]{0,1:T(8,128)S(1)}, s32[64,32]{0,1:T(8,128)}, u32[]{:S(2)}) copy-start(s32[64,32]{0,1:T(8,128)} %param.8) | copy-start | bytes 24580
  0.6 20.8 %collective-permute-start.3 = (f32[8,3,128]{2,0,1:T(8,128)}, f32[8,3,128]{2,0,1:T(8,128)S(1)}, u32[]{:S(2)}, u32[]{:S(2)}) collective-permute-start(f32[8,3,128]{2,0,1:T(8,128)} %param.9), channel_id=1, source_target_pairs={{0,4},{4,0},{8,12},{12,8},{1,5},{5,1},{9,13},{13,9},{2,6},{6,2},{1... | collective-permute-start | bytes 36872 | tf_op jit(solution)/shard_map/ppermute | solution.py:240
  0.7 20.8 %collective-permute-start.4 = (f32[8,3,128]{2,0,1:T(8,128)}, f32[8,3,128]{2,0,1:T(8,128)S(1)}, u32[]{:S(2)}, u32[]{:S(2)}) collective-permute-start(f32[8,3,128]{2,0,1:T(8,128)} %param.9), channel_id=1, source_target_pairs={{0,8},{4,12},{8,0},{12,4},{1,9},{5,13},{9,1},{13,5},{2,10},{6,14},... | collective-permute-start | bytes 36872 | tf_op jit(solution)/shard_map/ppermute | solution.py:240
  3.7 17.8 %collective-permute-start.5 = (f32[8,3,128]{2,0,1:T(8,128)}, f32[8,3,128]{2,0,1:T(8,128)S(1)}, u32[]{:S(2)}, u32[]{:S(2)}) collective-permute-start(f32[8,3,128]{2,0,1:T(8,128)} %param.9), channel_id=1, source_target_pairs={{0,12},{4,8},{8,4},{12,0},{1,13},{5,9},{9,5},{13,1},{2,14},{6,10},... | collective-permute-start | bytes 36872 | tf_op jit(solution)/shard_map/ppermute | solution.py:240
  21.5 0.6 copy-start.2
  46.3 50.0 %collective-permute-start.21 = (f32[4,32,128]{2,1,0:T(8,128)}, f32[4,32,128]{2,1,0:T(8,128)S(1)}, u32[]{:S(2)}, u32[]{:S(2)}) collective-permute-start(f32[4,32,128]{2,1,0:T(8,128)} %get-tuple-element.22), channel_id=1, source_target_pairs={{0,1},{1,0},{2,3},{3,2},{4,5},{5,4},{6,7},{7,6},{8,9},{9,8},{10,11... | collective-permute-start | bytes 196616 | tf_op jit(solution)/shard_map/ppermute | solution.py:240
  62.6 35.3 %collective-permute-start.16 = (f32[4,32,128]{2,1,0:T(8,128)}, f32[4,32,128]{2,1,0:T(8,128)S(1)}, u32[]{:S(2)}, u32[]{:S(2)}) collective-permute-start(f32[4,32,128]{2,1,0:T(8,128)} %get-tuple-element.20), channel_id=1, source_target_pairs={{0,1},{1,0},{2,3},{3,2},{4,5},{5,4},{6,7},{7,6},{8,9},{9,8},{10,11... | collective-permute-start | bytes 196616 | tf_op jit(solution)/shard_map/ppermute | solution.py:240
  79.4 19.1 %collective-permute-start.11 = (f32[4,32,128]{2,1,0:T(8,128)}, f32[4,32,128]{2,1,0:T(8,128)S(1)}, u32[]{:S(2)}, u32[]{:S(2)}) collective-permute-start(f32[4,32,128]{2,1,0:T(8,128)} %get-tuple-element.18), channel_id=1, source_target_pairs={{0,1},{1,0},{2,3},{3,2},{4,5},{5,4},{6,7},{7,6},{8,9},{9,8},{10,11... | collective-permute-start | bytes 196616 | tf_op jit(solution)/shard_map/ppermute | solution.py:240
  79.5 16.9 %copy-start.5 = (f32[4,32,128]{2,1,0:T(8,128)S(1)}, f32[4,32,128]{2,1,0:T(8,128)}, u32[]{:S(2)}) copy-start(f32[4,32,128]{2,1,0:T(8,128)} %get-tuple-element.21) | copy-start | bytes 196612
  79.5 18.4 %copy-start.4 = (f32[4,32,128]{2,1,0:T(8,128)S(1)}, f32[4,32,128]{2,1,0:T(8,128)}, u32[]{:S(2)}) copy-start(f32[4,32,128]{2,1,0:T(8,128)} %get-tuple-element.19) | copy-start | bytes 196612
  79.5 19.1 %copy-start.3 = (f32[4,32,128]{2,1,0:T(8,128)S(1)}, f32[4,32,128]{2,1,0:T(8,128)}, u32[]{:S(2)}) copy-start(f32[4,32,128]{2,1,0:T(8,128)} %get-tuple-element.17) | copy-start | bytes 196612
  79.5 30.6 %copy-start.7 = (s32[8,4]{0,1:T(4,128)S(1)}, s32[8,4]{0,1:T(4,128)}, u32[]{:S(2)}) copy-start(s32[8,4]{0,1:T(4,128)} %param.10) | copy-start | bytes 388
  95.8 4.3 %collective-permute-start.6 = (f32[4,32,128]{2,1,0:T(8,128)}, f32[4,32,128]{2,1,0:T(8,128)S(1)}, u32[]{:S(2)}, u32[]{:S(2)}) collective-permute-start(f32[4,32,128]{2,1,0:T(8,128)} %get-tuple-element.16), channel_id=1, source_target_pairs={{0,1},{1,0},{2,3},{3,2},{4,5},{5,4},{6,7},{7,6},{8,9},{9,8},{10,11... | collective-permute-start | bytes 196616 | tf_op jit(solution)/shard_map/ppermute | solution.py:240
  96.3 5.2 %collective-permute-start.22 = (f32[4,32,128]{2,1,0:T(8,128)S(1)}, f32[4,32,128]{2,1,0:T(8,128)S(1)}, u32[]{:S(2)}, u32[]{:S(2)}) collective-permute-start(f32[4,32,128]{2,1,0:T(8,128)S(1)} %add.87), channel_id=1, source_target_pairs={{0,2},{2,0},{1,3},{3,1},{4,6},{6,4},{5,7},{7,5},{8,10},{10,8},{9,1... | collective-permute-start | bytes 196616 | tf_op jit(solution)/shard_map/ppermute | solution.py:240
  97.9 4.9 %collective-permute-start.17 = (f32[4,32,128]{2,1,0:T(8,128)S(1)}, f32[4,32,128]{2,1,0:T(8,128)S(1)}, u32[]{:S(2)}, u32[]{:S(2)}) collective-permute-start(f32[4,32,128]{2,1,0:T(8,128)S(1)} %add.83), channel_id=1, source_target_pairs={{0,2},{2,0},{1,3},{3,1},{4,6},{6,4},{5,7},{7,5},{8,10},{10,8},{9,1... | collective-permute-start | bytes 196616 | tf_op jit(solution)/shard_map/ppermute | solution.py:240
  98.5 17.1 %copy-start.1 = (f32[8,128,128]{2,1,0:T(8,128)S(1)}, f32[8,128,128]{2,1,0:T(8,128)}, u32[]{:S(2)}) copy-start(f32[8,128,128]{2,1,0:T(8,128)} %param.11) | copy-start | bytes 1572868
  98.5 5.6 %collective-permute-start.12 = (f32[4,32,128]{2,1,0:T(8,128)S(1)}, f32[4,32,128]{2,1,0:T(8,128)S(1)}, u32[]{:S(2)}, u32[]{:S(2)}) collective-permute-start(f32[4,32,128]{2,1,0:T(8,128)S(1)} %add.79), channel_id=1, source_target_pairs={{0,2},{2,0},{1,3},{3,1},{4,6},{6,4},{5,7},{7,5},{8,10},{10,8},{9,1... | collective-permute-start | bytes 196616 | tf_op jit(solution)/shard_map/ppermute | solution.py:240
  101.0 4.3 %collective-permute-start.7 = (f32[4,32,128]{2,1,0:T(8,128)S(1)}, f32[4,32,128]{2,1,0:T(8,128)S(1)}, u32[]{:S(2)}, u32[]{:S(2)}) collective-permute-start(f32[4,32,128]{2,1,0:T(8,128)S(1)} %add.75), channel_id=1, source_target_pairs={{0,2},{2,0},{1,3},{3,1},{4,6},{6,4},{5,7},{7,5},{8,10},{10,8},{9,1... | collective-permute-start | bytes 196616 | tf_op jit(solution)/shard_map/ppermute | solution.py:240
  101.6 5.1 %collective-permute-start.23 = (f32[4,32,128]{2,1,0:T(8,128)S(1)}, f32[4,32,128]{2,1,0:T(8,128)S(1)}, u32[]{:S(2)}, u32[]{:S(2)}) collective-permute-start(f32[4,32,128]{2,1,0:T(8,128)S(1)} %add.88), channel_id=1, source_target_pairs={{0,4},{4,0},{8,12},{12,8},{1,5},{5,1},{9,13},{13,9},{2,6},{6,2},{1... | collective-permute-start | bytes 196616 | tf_op jit(solution)/shard_map/ppermute | solution.py:240
  102.8 8.2 %collective-permute-start.18 = (f32[4,32,128]{2,1,0:T(8,128)S(1)}, f32[4,32,128]{2,1,0:T(8,128)S(1)}, u32[]{:S(2)}, u32[]{:S(2)}) collective-permute-start(f32[4,32,128]{2,1,0:T(8,128)S(1)} %add.84), channel_id=1, source_target_pairs={{0,4},{4,0},{8,12},{12,8},{1,5},{5,1},{9,13},{13,9},{2,6},{6,2},{1... | collective-permute-start | bytes 196616 | tf_op jit(solution)/shard_map/ppermute | solution.py:240
  104.1 7.0 %collective-permute-start.13 = (f32[4,32,128]{2,1,0:T(8,128)S(1)}, f32[4,32,128]{2,1,0:T(8,128)S(1)}, u32[]{:S(2)}, u32[]{:S(2)}) collective-permute-start(f32[4,32,128]{2,1,0:T(8,128)S(1)} %add.80), channel_id=1, source_target_pairs={{0,4},{4,0},{8,12},{12,8},{1,5},{5,1},{9,13},{13,9},{2,6},{6,2},{1... | collective-permute-start | bytes 196616 | tf_op jit(solution)/shard_map/ppermute | solution.py:240
  105.3 8.8 %collective-permute-start.8 = (f32[4,32,128]{2,1,0:T(8,128)S(1)}, f32[4,32,128]{2,1,0:T(8,128)S(1)}, u32[]{:S(2)}, u32[]{:S(2)}) collective-permute-start(f32[4,32,128]{2,1,0:T(8,128)S(1)} %add.76), channel_id=1, source_target_pairs={{0,4},{4,0},{8,12},{12,8},{1,5},{5,1},{9,13},{13,9},{2,6},{6,2},{1... | collective-permute-start | bytes 196616 | tf_op jit(solution)/shard_map/ppermute | solution.py:240
  106.7 8.5 %collective-permute-start.24 = (f32[4,32,128]{2,1,0:T(8,128)S(1)}, f32[4,32,128]{2,1,0:T(8,128)S(1)}, u32[]{:S(2)}, u32[]{:S(2)}) collective-permute-start(f32[4,32,128]{2,1,0:T(8,128)S(1)} %add.89), channel_id=1, source_target_pairs={{0,8},{4,12},{8,0},{12,4},{1,9},{5,13},{9,1},{13,5},{2,10},{6,14},... | collective-permute-start | bytes 196616 | tf_op jit(solution)/shard_map/ppermute | solution.py:240
  110.0 5.7 %collective-permute-start = (s32[8,4]{0,1:T(4,128)S(1)}, s32[8,4]{0,1:T(4,128)S(1)}, u32[]{:S(2)}, u32[]{:S(2)}) collective-permute-start(s32[8,4]{0,1:T(4,128)S(1)} %copy-done.7), channel_id=1, source_target_pairs={{0,4},{4,0},{8,12},{12,8},{1,5},{5,1},{9,13},{13,9},{2,6},{6,2},{1... | collective-permute-start | bytes 392 | tf_op jit(solution)/shard_map/ppermute | solution.py:240
  111.0 17.8 %collective-permute-start.19 = (f32[4,32,128]{2,1,0:T(8,128)S(1)}, f32[4,32,128]{2,1,0:T(8,128)S(1)}, u32[]{:S(2)}, u32[]{:S(2)}) collective-permute-start(f32[4,32,128]{2,1,0:T(8,128)S(1)} %add.85), channel_id=1, source_target_pairs={{0,8},{4,12},{8,0},{12,4},{1,9},{5,13},{9,1},{13,5},{2,10},{6,14},... | collective-permute-start | bytes 196616 | tf_op jit(solution)/shard_map/ppermute | solution.py:240
  111.2 18.6 %collective-permute-start.14 = (f32[4,32,128]{2,1,0:T(8,128)S(1)}, f32[4,32,128]{2,1,0:T(8,128)S(1)}, u32[]{:S(2)}, u32[]{:S(2)}) collective-permute-start(f32[4,32,128]{2,1,0:T(8,128)S(1)} %add.81), channel_id=1, source_target_pairs={{0,8},{4,12},{8,0},{12,4},{1,9},{5,13},{9,1},{13,5},{2,10},{6,14},... | collective-permute-start | bytes 196616 | tf_op jit(solution)/shard_map/ppermute | solution.py:240
  114.1 16.4 %collective-permute-start.9 = (f32[4,32,128]{2,1,0:T(8,128)S(1)}, f32[4,32,128]{2,1,0:T(8,128)}, u32[]{:S(2)}, u32[]{:S(2)}) collective-permute-start(f32[4,32,128]{2,1,0:T(8,128)S(1)} %add.77), channel_id=1, source_target_pairs={{0,8},{4,12},{8,0},{12,4},{1,9},{5,13},{9,1},{13,5},{2,10},{6,14},... | collective-permute-start | bytes 196616 | tf_op jit(solution)/shard_map/ppermute | solution.py:240
  115.3 16.1 %collective-permute-start.25 = (f32[4,32,128]{2,1,0:T(8,128)S(1)}, f32[4,32,128]{2,1,0:T(8,128)}, u32[]{:S(2)}, u32[]{:S(2)}) collective-permute-start(f32[4,32,128]{2,1,0:T(8,128)S(1)} %add.90), channel_id=1, source_target_pairs={{0,1},{1,0},{2,3},{3,2},{4,5},{5,4},{6,7},{7,6},{8,9},{9,8},{10,11... | collective-permute-start | bytes 196616 | tf_op jit(solution)/shard_map/ppermute | solution.py:240
  115.7 5.0 %collective-permute-start.1 = (s32[8,4]{0,1:T(4,128)S(1)}, s32[8,4]{0,1:T(4,128)S(1)}, u32[]{:S(2)}, u32[]{:S(2)}) collective-permute-start(s32[8,4]{0,1:T(4,128)S(1)} %copy-done.7), channel_id=1, source_target_pairs={{0,8},{4,12},{8,0},{12,4},{1,9},{5,13},{9,1},{13,5},{2,10},{6,14},... | collective-permute-start | bytes 392 | tf_op jit(solution)/shard_map/ppermute | solution.py:240
  120.7 3.6 %collective-permute-start.2 = (s32[8,4]{0,1:T(4,128)S(1)}, s32[8,4]{0,1:T(4,128)S(1)}, u32[]{:S(2)}, u32[]{:S(2)}) collective-permute-start(s32[8,4]{0,1:T(4,128)S(1)} %copy-done.7), channel_id=1, source_target_pairs={{0,12},{4,8},{8,4},{12,0},{1,13},{5,9},{9,5},{13,1},{2,14},{6,10},... | collective-permute-start | bytes 392 | tf_op jit(solution)/shard_map/ppermute | solution.py:240
  124.3 22.3 %collective-permute-start.26 = (f32[8,128,128]{2,1,0:T(8,128)S(1)}, f32[8,128,128]{2,1,0:T(8,128)S(1)}, u32[]{:S(2)}, u32[]{:S(2)}) collective-permute-start(f32[8,128,128]{2,1,0:T(8,128)S(1)} %copy-done.1), channel_id=1, source_target_pairs={{0,4},{4,0},{8,12},{12,8},{1,5},{5,1},{9,13},{13,9},{2,6},{6,2},{1... | collective-permute-start | bytes 1572872 | tf_op jit(solution)/shard_map/ppermute | solution.py:240
  128.8 35.8 %collective-permute-start.27 = (f32[8,128,128]{2,1,0:T(8,128)S(1)}, f32[8,128,128]{2,1,0:T(8,128)S(1)}, u32[]{:S(2)}, u32[]{:S(2)}) collective-permute-start(f32[8,128,128]{2,1,0:T(8,128)S(1)} %copy-done.1), channel_id=1, source_target_pairs={{0,8},{4,12},{8,0},{12,4},{1,9},{5,13},{9,1},{13,5},{2,10},{6,14},... | collective-permute-start | bytes 1572872 | tf_op jit(solution)/shard_map/ppermute | solution.py:240
  129.8 44.7 %collective-permute-start.28 = (f32[8,128,128]{2,1,0:T(8,128)S(1)}, f32[8,128,128]{2,1,0:T(8,128)S(1)}, u32[]{:S(2)}, u32[]{:S(2)}) collective-permute-start(f32[8,128,128]{2,1,0:T(8,128)S(1)} %copy-done.1), channel_id=1, source_target_pairs={{0,12},{4,8},{8,4},{12,0},{1,13},{5,9},{9,5},{13,1},{2,14},{6,10},... | collective-permute-start | bytes 1572872 | tf_op jit(solution)/shard_map/ppermute | solution.py:240
  130.5 3.0 %collective-permute-start.20 = (f32[4,32,128]{2,1,0:T(8,128)S(1)}, f32[4,32,128]{2,1,0:T(8,128)S(1)}, u32[]{:S(2)}, u32[]{:S(2)}) collective-permute-start(f32[4,32,128]{2,1,0:T(8,128)S(1)} %add.86), channel_id=1, source_target_pairs={{0,1},{1,0},{2,3},{3,2},{4,5},{5,4},{6,7},{7,6},{8,9},{9,8},{10,11... | collective-permute-start | bytes 196616 | tf_op jit(solution)/shard_map/ppermute | solution.py:240
  131.4 2.8 %collective-permute-start.15 = (f32[4,32,128]{2,1,0:T(8,128)S(1)}, f32[4,32,128]{2,1,0:T(8,128)S(1)}, u32[]{:S(2)}, u32[]{:S(2)}) collective-permute-start(f32[4,32,128]{2,1,0:T(8,128)S(1)} %add.82), channel_id=1, source_target_pairs={{0,1},{1,0},{2,3},{3,2},{4,5},{5,4},{6,7},{7,6},{8,9},{9,8},{10,11... | collective-permute-start | bytes 196616 | tf_op jit(solution)/shard_map/ppermute | solution.py:240
  133.5 1.4 collective-permute-start.10
  174.5 1.4 copy-start

commit v2 on v0

v2 whole, which is shorter than its diff:
```python
import functools
import math

import jax
import jax.numpy as jnp
from jax import lax
from jax.experimental import pallas as pl
from jax.experimental.pallas import tpu as pltpu
from jax.sharding import PartitionSpec as P

SWEEPS = 2
RADIUS = 1.2
SCALE = 4.0 / RADIUS
GEO = 32
TILE = 4
STEPS = 4
f32, bf16 = jnp.float32, jnp.bfloat16
VMEM = pl.BlockSpec(memory_space=pltpu.VMEM)
SMEM = pl.BlockSpec(memory_space=pltpu.SMEM)
ANY = pl.BlockSpec(memory_space=pl.ANY)
HBM = pl.BlockSpec(memory_space=pltpu.HBM)


def call(kernel, name, out, scratch, operands, specs, cost=None):
    size = 0
    for x in [*out, *scratch, *operands]:
        if len(x.shape) < 2:
            continue
        size += math.prod(x.shape[:-1]) * max(x.shape[-1], 128) * jnp.dtype(x.dtype).itemsize
    return pl.pallas_call(
        kernel,
        out_shape=out,
        in_specs=specs,
        out_specs=[VMEM] * len(out),
        scratch_shapes=scratch,
        compiler_params=pltpu.CompilerParams(vmem_limit_bytes=size + (4 << 20)),
        cost_estimate=cost,
        name=name,
    )(*operands)


def shape(dims, kind):
    return jax.ShapeDtypeStruct(dims, kind)


def root_of(square):
    root = jnp.maximum(square, 1e-12)
    return root * lax.rsqrt(root)


def split3(v):
    a = v.astype(bf16).astype(f32)
    b = (v - a).astype(bf16).astype(f32)
    return (a, b, v - a - b)


def pairs_of_parts():
    return [(a, b) for a in range(3) for b in range(3) if a + b < 4]


def left_rows(xyz):
    rows = []
    for v in xyz:
        parts = split3(v)
        rows += [parts[a] for a, b in pairs_of_parts()]
    rows += list(split3(sum(v * v for v in xyz)))
    return rows + [jnp.ones_like(xyz[0])] * 3


def right_rows(xyz):
    rows = []
    for v in xyz:
        parts = split3(v)
        rows += [-2.0 * parts[b] for a, b in pairs_of_parts()]
    rows += [jnp.ones_like(xyz[0])] * 3
    return rows + list(split3(sum(v * v for v in xyz)))


def place(whole, me, own, pieces):
    whole[me] = own[...] * SCALE
    for step, piece in enumerate(pieces, 1):
        whole[me ^ step] = piece[...] * SCALE


def some(whole, first, per):
    own = whole.shape[2]
    spans = []
    at = first
    while at < first + per:
        node, low = at // own, at % own
        high = min(own, low + first + per - at)
        spans.append((node, low, high))
        at += high - low
    return [
        jnp.concatenate([whole[node, d, low:high] for node, low, high in spans], axis=0)
        for d in range(3)
    ]


def fill_rows(scratch, rows):
    for g, row in enumerate(rows):
        scratch[:, g, :] = row
    for g in range(len(rows), scratch.shape[1]):
        scratch[:, g, :] = jnp.zeros_like(rows[0])


def prepare_kernel(
    controls, side_ref, volume_hbm, listed_hbm, grad_hbm, control_hbm, inverse_hbm, near_hbm, *refs
):
    left_ref, counts_ref, grad_ref, control_ref, parcel_ref = refs[:5]
    coords, listed, scratch, tally, inverse, near, sems = refs[5:]
    half = inverse.shape[0]
    mine = pl.ds(side_ref[0] * half, half)
    copies = [
        pltpu.make_async_copy(source, target, sems.at[n])
        for n, (source, target) in enumerate(
            [
                (volume_hbm, coords),
                (listed_hbm, listed),
                (inverse_hbm.at[mine], inverse),
                (near_hbm, near),
                (control_hbm, control_ref),
                (grad_hbm, grad_ref),
            ]
        )
    ]
    for copy in copies:
        copy.start()
    copies[0].wait()
    fill_rows(scratch, left_rows([coords[d] * SCALE for d in range(3)]))
    blocks, width, depth = left_ref.shape
    lane = lax.broadcasted_iota(jnp.int32, (width, depth), 1)

    def one(s, _):
        turned = scratch[s].T
        turned = jnp.concatenate([turned, jnp.zeros((width, depth - GEO), f32)], axis=1)
        left_ref[s] = jnp.where(lane == s + GEO, 1.0, turned).astype(bf16)
        return 0

    lax.fori_loop(0, blocks, one, 0, unroll=8)
    copies[1].wait()
    chosen = listed[...]
    tally[...] = jnp.zeros_like(tally)
    for c in range(controls):
        tally[c : c + 1, 0:blocks] = jnp.sum(
            jnp.where(chosen == c, 1.0, 0.0), axis=0, keepdims=True
        )
    counts_ref[...] = tally[...].T
    copies[2].wait()
    copies[3].wait()
    for q in range(half):
        parcel_ref[q * 128 : (q + 1) * 128] = inverse[q].astype(bf16)
    tail = jnp.concatenate(
        [
            near[...].astype(f32),
            jnp.zeros((near.shape[0], width - near.shape[1]), f32),
        ],
        axis=1,
    )
    tail = jnp.concatenate([tail, jnp.zeros((16 - near.shape[0], width), f32)], axis=0)
    parcel_ref[half * 128 :] = tail.astype(bf16)
    copies[4].wait()
    copies[5].wait()


def chunk_kernel(first, per, copied, waits, nodes, listed, *refs):
    refs = list(refs)

    def take(n):
        taken = refs[:n]
        del refs[:n]
        return taken

    side_ref, me_ref, left_ref, grad_ref, counts_ref = take(5)
    pieces = take(nodes)
    before = take(2 * (copied > 0))
    take(waits)
    keep_ref, send_ref = take(2)
    coords, features, rhs, total, result, d0, d1, p0, p1 = refs
    blocks = grad_ref.shape[0]
    depth = rhs.shape[1]
    steps = blocks // TILE
    pairs = per // 2
    whole = pairs * steps
    size = TILE * 128
    counts = counts_ref[0:blocks, first : first + per].astype(jnp.int32)
    most = jnp.max(counts)
    layers = jnp.int32(0)
    for b in range(listed.bit_length()):
        layers = layers + jnp.where(most >= (1 << b), 1, 0)
    result[...] = jnp.zeros_like(result)
    place(coords, me_ref[0], pieces[0], pieces[1:])
    fill_rows(features, right_rows(some(coords, first, per)))
    rhs[...] = jnp.zeros_like(rhs)
    for c in range(per):
        rhs[c // 2, 0:GEO, (c % 2) * 128 : (c % 2 + 1) * 128] = features[c].astype(bf16)

    def distances(t, d):
        j, i = t // steps, t % steps
        left = left_ref[pl.ds(i * TILE, TILE)].reshape(size, depth)
        d[...] = jnp.dot(left, rhs[j], preferred_element_type=f32)

    def values(d, p):
        root = root_of(d[...])
        inside = jnp.maximum(4.0 - root, 0.0)
        twice = inside * inside
        p[0:size] = (twice * twice).astype(bf16)
        p[size:] = root.astype(bf16)

    def products(t, p):
        j, i = t // steps, t % steps
        g = jnp.concatenate([grad_ref[i * TILE + q] for q in range(TILE)], axis=1)
        even, odd = p[0:size], p[0:size] * p[size:]
        total[j] += (
            jnp.dot(g, even, preferred_element_type=f32)
            + jnp.dot(g, odd, preferred_element_type=f32)
        )

    def layer(b, weight):
        for c in range(per):
            bit = jnp.bitwise_and(lax.shift_right_logical(counts[:, c : c + 1], b), 1)
            far = jnp.where(jnp.broadcast_to(bit, (blocks, 128)) == 1, 0.0, 65536.0)
            rhs[c // 2, GEO : GEO + blocks, (c % 2) * 128 : (c % 2 + 1) * 128] = far.astype(bf16)
        total[...] = jnp.zeros_like(total)
        p1[...] = jnp.zeros_like(p1)
        distances(0, d0)

        def turn(h, _):
            for u in range(STEPS):
                t = STEPS * h + u
                d, p = (d0, p0) if u % 2 == 0 else (d1, p1)
                later, done = (d1, p1) if u % 2 == 0 else (d0, p0)
                values(d, p)
                products(jnp.maximum(t - 1, 0), done)
                distances(jnp.minimum(t + 1, whole - 1), later)
            return 0

        lax.fori_loop(0, whole // STEPS, turn, 0)
        products(whole - 1, p1)
        result[...] += weight * total[...]
        return weight * 2.0

    lax.fori_loop(0, layers, layer, jnp.float32(1.0 / 256.0))
    side = side_ref[0]
    if before:
        keep_ref[0:copied] = before[0][...]
        send_ref[0:copied] = before[1][...]
    half = pairs // 2
    for j in range(half):
        mine = result[side * half + j]
        other = result[(1 - side) * half + j]
        for q in range(2):
            keep_ref[copied + 2 * j + q] = mine[:, q * 128 : (q + 1) * 128]
            send_ref[copied + 2 * j + q] = other[:, q * 128 : (q + 1) * 128]


def features_kernel(nodes, waits, *refs):
    side_ref, me_ref, inverse_ref = refs[:3]
    pieces = refs[3 : 3 + nodes]
    parcels = refs[3 + nodes : 3 + nodes + 2 * (nodes - 1)]
    left_ref, right_ref, high_ref, low_ref, coords, features = refs[-6:]
    own = inverse_ref.shape[0]
    half = own // 2
    side, me = side_ref[0], me_ref[0]
    for c in range(own):
        inv = inverse_ref[c]
        high = inv.astype(bf16)
        at = (c % 2) * 128
        high_ref[me * half + c // 2, :, at : at + 128] = high
        low_ref[c // 2, :, at : at + 128] = (inv - high.astype(f32)).astype(bf16)
    for step in range(1, nodes):
        for whose in range(2):
            parcel = parcels[whose * (nodes - 1) + step - 1]
            core = (1 - 2 * whose) * side + whose
            for c in range(half):
                pair = (me ^ step) * half + core * (half // 2) + c // 2
                at = (c % 2) * 128
                high_ref[pair, :, at : at + 128] = parcel[c * 128 : (c + 1) * 128]

    place(coords, me, pieces[0], pieces[1:])
    blocks = left_ref.shape[0]
    xyz = some(coords, 0, blocks)
    fill_rows(features, right_rows(xyz))
    right_ref[...] = features[...].astype(bf16)
    fill_rows(features, left_rows(xyz))

    def turn_left(c, _):
        left_ref[c] = features[c].T.astype(bf16)
        return 0

    lax.fori_loop(0, blocks, turn_left, 0, unroll=8)


def pairs_kernel(near_ref, left_ref, right_ref, *refs):
    phi_ref, d0, d1 = refs[-3:]
    blocks = right_ref.shape[0]
    _, coupled, own = near_ref.shape

    def distances(c, d):
        points = [left_ref[near_ref[c // own, k, c % own]] for k in range(coupled)]
        d[...] = jnp.dot(jnp.concatenate(points, axis=0), right_ref[c], preferred_element_type=f32)

    def values(pair, q, d):
        root = root_of(d[...])
        inside = jnp.maximum(1.0 - 0.25 * root, 0.0)
        twice = inside * inside
        phi_ref[pair, :, q * 128 : (q + 1) * 128] = ((twice * twice) * (1.0 + root)).astype(bf16)

    distances(0, d0)

    def turn(h, _):
        for u in range(STEPS):
            c = STEPS * h + u
            values(2 * h + u // 2, u % 2, d0 if u % 2 == 0 else d1)
            distances(jnp.minimum(c + 1, blocks - 1), d1 if u % 2 == 0 else d0)
        return 0

    lax.fori_loop(0, blocks // STEPS, turn, 0)


def add_kernel(x_ref, y_ref, *refs):
    refs[-1][...] = x_ref[...] + y_ref[...]


def solve_kernel(chains, *refs):
    side_ref, me_ref, near_ref = refs[:3]
    halves = refs[3 : 3 + 2 * len(chains)]
    phi_ref, high_ref, low_ref, grad_out, adjoint_out, grads, values0, values1 = refs[
        3 + 2 * len(chains) :
    ]
    pairs = high_ref.shape[0]
    _, coupled, own = near_ref.shape
    side = side_ref[0]
    for n, groups in enumerate(chains):
        at = 0
        for first, per in groups:
            half = per // 2
            grads[pl.ds(first + side * half, half)] = halves[2 * n][at : at + half]
            grads[pl.ds(first + (1 - side) * half, half)] = halves[2 * n + 1][at : at + half]
            at += half

    def through(two, weights, exact):
        rows = []
        for x in two:
            high = x.astype(bf16)
            low = (x - high.astype(f32)).astype(bf16)
            rows.append(jnp.concatenate([high, high], axis=1) if exact else high)
            rows.append(jnp.concatenate([low, jnp.zeros_like(low)], axis=1) if exact else low)
        out = jnp.dot(jnp.concatenate(rows, axis=0), weights, preferred_element_type=f32)
        n = two[0].shape[0]
        return [
            out[2 * q * n : (2 * q + 1) * n, q * 128 : (q + 1) * 128]
            + out[(2 * q + 1) * n : (2 * q + 2) * n, q * 128 : (q + 1) * 128]
            for q in range(2)
        ]

    def start(pair, _):
        done = through([grads[2 * pair], grads[2 * pair + 1]], high_ref[pair], False)
        for q in range(2):
            values0[2 * pair + q] = done[q].astype(bf16)
        return 0

    lax.fori_loop(0, pairs, start, 0, unroll=8)

    def rest(old, pair):
        near = []
        for q in range(2):
            c = 2 * pair + q
            near.append(
                jnp.concatenate(
                    [old[near_ref[c // own, k, c % own]] for k in range(coupled)], axis=1
                )
            )
        n = near[0].shape[0]
        coupling = jnp.dot(
            jnp.concatenate(near, axis=0), phi_ref[pair], preferred_element_type=f32
        )
        return [
            grads[2 * pair + q] - coupling[q * n : (q + 1) * n, q * 128 : (q + 1) * 128]
            for q in range(2)
        ]

    old, new = values0, values1
    for sweep in range(SWEEPS - 1):
        def one(pair, _, old=old, new=new):
            done = through(rest(old, pair), high_ref[pair], False)
            for q in range(2):
                new[2 * pair + q] = done[q].astype(bf16)
            return 0

        lax.fori_loop(0, pairs, one, 0, unroll=8)
        old, new = new, old

    first = me_ref[0] * (own // 2)
    for pair in range(own // 2):
        weights = jnp.concatenate([high_ref[first + pair], low_ref[pair]], axis=0)
        done = through(rest(old, first + pair), weights, True)
        for q in range(2):
            grad_out[2 * pair + q] = grads[2 * (first + pair) + q]
            adjoint_out[2 * pair + q] = done[q]


def exchange(x, axis, size, step):
    return lax.ppermute(x, axis, [(i, i ^ step) for i in range(size)])


def doubling(size):
    return [1 << b for b in range(size.bit_length() - 1)]


def local(sizes, volume_grad, volume_coords, support, control_coords, neighbours, block_inverse):
    nodes, fns, subs = sizes["node"], sizes["fn"], sizes["sub"]
    blocks, funcs, width = volume_grad.shape
    own, coupled = neighbours.shape
    controls = own * nodes
    depth = -(-(blocks + GEO) // 128) * 128
    side = lax.axis_index("sub").astype(jnp.int32).reshape(1)
    me = lax.axis_index("node").astype(jnp.int32).reshape(1)

    coords = control_coords.transpose(1, 0, 2)
    pieces = [exchange(coords, "node", nodes, step) for step in range(1, nodes)]
    left, counts, grads, own_coords, parcel = call(
        functools.partial(prepare_kernel, controls),
        "prepare",
        [
            shape((blocks, width, depth), bf16),
            shape((width, width), f32),
            shape(volume_grad.shape, volume_grad.dtype),
            shape(coords.shape, f32),
            shape((own // 2 * width + 16, width), bf16),
        ],
        [
            pltpu.VMEM((3, blocks, width), f32),
            pltpu.VMEM(support.T.shape, jnp.int32),
            pltpu.VMEM((blocks, GEO, width), f32),
            pltpu.VMEM((width, width), f32),
            pltpu.VMEM((own // 2, width, width), f32),
            pltpu.VMEM((coupled, own), jnp.int32),
            pltpu.SemaphoreType.DMA((6,)),
        ],
        [
            side,
            volume_coords.transpose(1, 0, 2),
            support.T,
            volume_grad,
            coords,
            block_inverse,
            neighbours.T,
        ],
        [SMEM] + [HBM] * 6,
    )
    pieces = [own_coords] + pieces
    parcels = [exchange(parcel, "node", nodes, step) for step in range(1, nodes)]

    def evaluate(first, per, before, after):
        entries = blocks * per * width * width
        copied = before[0].shape[0] if before else 0
        operands = [side, me, left, grads, counts, *pieces, *before]
        out = [shape((copied + per // 2, funcs, width), f32)] * 2
        return call(
            functools.partial(
                chunk_kernel,
                first,
                per,
                copied,
                len(after),
                nodes,
                support.shape[1],
            ),
            f"evaluate_{first}",
            out,
            [
                pltpu.VMEM((nodes, 3, own, width), f32),
                pltpu.VMEM((per, GEO, width), f32),
                pltpu.VMEM((per // 2, depth, 2 * width), bf16),
                pltpu.VMEM((per // 2, funcs, 2 * width), f32),
                pltpu.VMEM((per // 2, funcs, 2 * width), f32),
                pltpu.VMEM((TILE * width, 2 * width), f32),
                pltpu.VMEM((TILE * width, 2 * width), f32),
                pltpu.VMEM((2 * TILE * width, 2 * width), bf16),
                pltpu.VMEM((2 * TILE * width, 2 * width), bf16),
            ],
            operands + after,
            [SMEM, SMEM] + [VMEM] * (len(operands) - 2) + [ANY] * len(after),
            pl.CostEstimate(flops=entries * 400, bytes_accessed=4 << 20, transcendentals=entries),
        )

    def add(x, y, after):
        return call(
            add_kernel,
            "add",
            [shape(x.shape, x.dtype)],
            [],
            [x, y, *after],
            [VMEM, VMEM] + [ANY] * len(after),
        )[0]

    eighth = controls // 8
    groups = [(0, 4 * eighth)] + [((4 + n) * eighth, eighth) for n in range(4)]
    chains = [groups[:1], groups[1:3], groups[3:]]

    def over_node(x):
        for step in doubling(nodes):
            x = add(x, exchange(x, "node", nodes, step), [])
        return x

    def over_fn(x):
        for step in doubling(fns):
            x = add(x, exchange(x, "fn", fns, step), [])
        return x

    keep, send = evaluate(*groups[0], [], [])
    a0 = add(keep, exchange(send, "sub", subs, 1), [])
    one = evaluate(*groups[1], [], [send])
    a1 = over_fn(a0)
    theirs = [exchange(piece, "sub", subs, 1) for piece in parcels]
    two = evaluate(*groups[2], list(one), [a0])
    steps = doubling(nodes)
    a2 = a1
    for step in steps[: len(steps) // 2]:
        a2 = add(a2, exchange(a2, "node", nodes, step), [])
    b0 = add(two[0], exchange(two[1], "sub", subs, 1), [])
    three = evaluate(*groups[3], [], [a1, two[1]])
    a3 = a2
    for step in steps[len(steps) // 2 :]:
        a3 = add(a3, exchange(a3, "node", nodes, step), [])
    b1 = over_fn(b0)
    four = evaluate(*groups[4], list(three), [a2, b0])
    a4 = exchange(a3, "sub", subs, 1)
    b2 = over_node(b1)
    b3 = exchange(b2, "sub", subs, 1)
    c0 = add(four[0], exchange(four[1], "sub", subs, 1), [])

    rows = own // 2 * width
    near = jnp.zeros((nodes, coupled, own), jnp.int32)
    near = lax.dynamic_update_index_in_dim(near, neighbours.T, me[0], 0)
    for step in range(1, nodes):
        told = parcels[step - 1][rows : rows + coupled, :own].astype(jnp.int32)
        near = lax.dynamic_update_index_in_dim(near, told, me[0] ^ step, 0)
    operands = [side, me, block_inverse, *pieces, *parcels, *theirs]
    control_left, control_right, high, low = call(
        functools.partial(features_kernel, nodes, 1),
        "control_features",
        [
            shape((controls, width, GEO), bf16),
            shape((controls, GEO, width), bf16),
            shape((controls // 2, width, 2 * width), bf16),
            shape((own // 2, width, 2 * width), bf16),
        ],
        [
            pltpu.VMEM((nodes, 3, own, width), f32),
            pltpu.VMEM((controls, GEO, width), f32),
        ],
        operands + [c0],
        [SMEM, SMEM] + [VMEM] * (len(operands) - 2) + [ANY],
        pl.CostEstimate(flops=10 << 30, bytes_accessed=1 << 20, transcendentals=0),
    )
    c1 = c0
    for step in doubling(fns):
        c1 = add(c1, exchange(c1, "fn", fns, step), [high])
    (phi,) = call(
        pairs_kernel,
        "pairs",
        [shape((controls // 2, coupled * width, 2 * width), bf16)],
        [
            pltpu.VMEM((coupled * width, width), f32),
            pltpu.VMEM((coupled * width, width), f32),
        ],
        [near, control_left, control_right, c1],
        [SMEM, VMEM, VMEM, ANY],
        pl.CostEstimate(flops=20 << 30, bytes_accessed=1 << 20, transcendentals=2 << 20),
    )
    c2 = c1
    for step in doubling(nodes):
        c2 = add(c2, exchange(c2, "node", nodes, step), [phi])
    c3 = exchange(c2, "sub", subs, 1)

    halves = [a3, a4, b2, b3, c2, c3]
    return tuple(
        call(
            functools.partial(solve_kernel, chains),
            "solve",
            [shape((own, funcs, width), f32)] * 2,
            [
                pltpu.VMEM((controls, funcs, width), f32),
                pltpu.VMEM((controls, funcs, width), bf16),
                pltpu.VMEM((controls, funcs, width), bf16),
            ],
            [side, me, near, *halves, phi, high, low],
            [SMEM, SMEM, SMEM] + [VMEM] * (len(halves) + 3),
        )
    )


def solution(mesh):
    return jax.shard_map(
        functools.partial(local, dict(mesh.shape)),
        mesh=mesh,
        in_specs=(
            P(("sect", "node", "fn", "sub"), None, None),
            P(("sect", "node", "fn", "sub"), None, None),
            P(("sect", "node", "fn", "sub"), None),
            P(("sect", "node"), None, None),
            P(("sect", "node"), None),
            P(("sect", "node"), None, None),
        ),
        out_specs=(P(("sect", "node"), None, None), P(("sect", "node"), None, None)),
        check_vma=False,
    )
```

time: 405 us -> 117 us (0.29)
  other arithmetic: 161 us -> 0.04 us
  matrix products: 102 us -> 0 us
  Pallas kernels: 0 us -> 74.5 us
  blocking collectives: 43 us -> 0 us
  waiting for transfers between devices: 48 us -> 9.7 us
  local copies, waits for them, and re-layouts: 31.8 us -> 5.78 us
  starting transfers between devices: 0.08 us -> 25.9 us
  between operations: 14.2 us -> 0.89 us
    dot_general x37 -> x0, matrix products: 102 us -> none  [the longest x32 97 us: step(): jnp.einsum('gfi,gkij->gkfj', block_grads, tiles_phi, preferred_element_ty...]
    scatter-add x32 -> x0, other arithmetic: 100 us -> none  [step(): total.at[block_lists.reshape(-1)].add(tiles.reshape(-1, funcs, width))]
    pallas_call x0 -> x21, Pallas kernels: none -> 74.5 us  [call(): pl.pallas_call(kernel, out_shape=out, in_specs=specs, out_specs=[VMEM] *...]
    reduce_sum x33 -> x0, other arithmetic: 57.5 us -> none  [wendland(): dist = jnp.sqrt(jnp.sum(diff * diff, axis=-3))]
    all_gather x3 -> x0, blocking collectives: 43 us -> none  [the longest x2 28 us: local(): lax.all_gather(adjoint.astype(jnp.bfloat16), 'node', axis=0, tiled=True)]
    psum x1 -> x0, waiting for transfers between devices: 29.3 us -> none  [local(): control_gradient = lax.psum(owned, ('fn', 'sub'))]
    ppermute x0 -> x24, starting transfers between devices: none -> 25.9 us  [exchange(): return lax.ppermute(x, axis, [(i, i ^ step) for i in range(size)])]
    gather x35 -> x0, local copies, waits for them, and re-layouts: 22.8 us -> none  [the longest x32 21 us: step(): centers = all_centers[block_lists]]
  transfers between devices with their start and end apart: 2 -> 24, of which waited for: 2 -> 5; matrix products, arithmetic and copies ran while one was open for 2% -> 1% of each run, Pallas kernels for 0% -> 59%
where the time goes in v2:
time: 117 us
  Pallas kernels  74.5 us (64%)
  starting transfers between devices  25.9 us (22%)
  waiting for transfers between devices  9.7 us (8%)
  local copies, waits for them, and re-layouts  5.78 us (5%)
    pallas_call x21, Pallas kernels, call(): pl.pallas_call(kernel, out_shape=out, in_specs=specs, out_specs=[VMEM] *...  74.5 us
    ppermute x24, starting transfers between devices, exchange(): return lax.ppermute(x, axis, [(i, i ^ step) for i in range(size)])  25.9 us
    ppermute x24, waiting for transfers between devices, exchange(): return lax.ppermute(x, axis, [(i, i ^ step) for i in range(size)])  9.7 us
    unnamed x14, local copies, waits for them, and re-layouts  5.09 us
  transfers between devices with their start and end apart: 24, of which 5 were waited for; matrix products, arithmetic and copies ran while one was open for 1% of the time, Pallas kernels for 59%

profile of v2, /device:TPU:0, one launch (start us, length us, event | category | flops | bytes accessed | tf_op | source)
XLA Modules:
  0.0 116.9 jit_solution(2657039312833161304)
XLA Ops:
  0.6 3.1 %collective-permute-start.3 = (f32[3,8,128]{2,1,0:T(8,128)}, f32[3,8,128]{2,1,0:T(8,128)S(1)}, u32[]{:S(2)}, u32[]{:S(2)}) collective-permute-start(f32[3,8,128]{2,1,0:T(8,128)} %bitcast.26), channel_id=1, source_target_pairs={{0,4},{4,0},{8,12},{12,8},{1,5},{5,1},{9,13},{13,9},{2,6},{6,2},{1... | collective-permute-start | bytes 36872 | tf_op jit(solution)/shard_map/ppermute | solution.py:404
  3.7 2.6 %collective-permute-start.4 = (f32[3,8,128]{2,1,0:T(8,128)}, f32[3,8,128]{2,1,0:T(8,128)S(1)}, u32[]{:S(2)}, u32[]{:S(2)}) collective-permute-start(f32[3,8,128]{2,1,0:T(8,128)} %bitcast.27), channel_id=1, source_target_pairs={{0,8},{4,12},{8,0},{12,4},{1,9},{5,13},{9,1},{13,5},{2,10},{6,14},... | collective-permute-start | bytes 36872 | tf_op jit(solution)/shard_map/ppermute | solution.py:404
  6.3 1.0 copy-done
  7.4 1.0 copy-done.1
  8.4 0.9 copy-done.3
  9.3 0.7 copy-done.4
  10.0 0.7 copy-done.5
  10.7 0.7 copy-done.6
  11.4 2.3 %prepare.1 = (bf16[64,128,128]{2,1,0:T(8,128)(2,1)S(1)}, f32[128,128]{1,0:T(8,128)S(1)}, bf16[64,32,128]{2,1,0:T(8,128)(2,1)S(1)}, f32[3,8,128]{2,1,0:T(8,128)S(1)}, bf16[528,128]{1,0:T(8,128)(2,1)S(1)}) custom-call(s32[1]{0:T(128)} %bitcast.side_ref.refs_0_, f32[3,64,128]{2,1,0:T(8,128)S(1)} %bitcast.24, s32[32,64]{1,0:T(8,128)S(1)} %bitcast.25, ...), custom_call_target="tpu_custom_call" | custom-call | tf_op jit(solution)/shard_map/prepare/pallas_call | solution.py:30
  13.7 1.0 collective-permute-start
  14.6 3.5 %collective-permute-start.1 = (bf16[528,128]{1,0:T(8,128)(2,1)S(1)}, bf16[528,128]{1,0:T(8,128)(2,1)S(1)}, u32[]{:S(2)}, u32[]{:S(2)}) collective-permute-start(bf16[528,128]{1,0:T(8,128)(2,1)S(1)} %get-tuple-element.21), channel_id=1, source_target_pairs={{0,8},{4,12},{8,0},{12,4},{1,9},{5,13},{9,1},{13,5},{2,10},{6,14},... | collective-permute-start | bytes 405512 | tf_op jit(solution)/shard_map/ppermute | solution.py:404
  18.1 0.7 bitcast_dynamic-update-slice_fusion
  18.8 0.0 collective-permute-done.3.refs_6_.refs_4_
  18.8 0.0 collective-permute-start.2
  18.8 0.0 collective-permute-done.4.refs_7_.refs_5_
  18.8 0.0 collective-permute-done.5.refs_8_.refs_6_
  18.8 28.6 %evaluate_0.1 = (f32[8,32,128]{2,1,0:T(8,128)S(1)}, f32[8,32,128]{2,1,0:T(8,128)S(1)}) custom-call(s32[1]{0:T(128)} %bitcast.side_ref.refs_0_, s32[1]{0:T(128)} %bitcast.1.refs_1_, bf16[64,128,128]{2,1,0:T(8,128)(2,1)S(1)} %get-tuple-element.22.refs_2_, bf16[64,32,128]{2,1,0:T(8,128)(2,1)S(1)} %get-tuple-element.23.refs_3_, ...), custom_call_target="tpu_custom_call" | custom-call | flops 6710886400 | bytes 4194304 | tf_op jit(solution)/shard_map/evaluate_0/pallas_call | solution.py:30
  47.5 0.1 collective-permute-start.6
  47.6 7.7 %evaluate_16.1 = (f32[2,32,128]{2,1,0:T(8,128)S(1)}, f32[2,32,128]{2,1,0:T(8,128)S(1)}) custom-call(s32[1]{0:T(128)} %bitcast.side_ref.refs_0_, s32[1]{0:T(128)} %bitcast.1.refs_1_, bf16[64,128,128]{2,1,0:T(8,128)(2,1)S(1)} %get-tuple-element.22.refs_2_, bf16[64,32,128]{2,1,0:T(8,128)(2,1)S(1)} %get-tuple-element.23.refs_3_, ...), custom_call_target="tpu_custom_call" | custom-call | flops 1677721600 | bytes 4194304 | tf_op jit(solution)/shard_map/evaluate_16/pallas_call | solution.py:30
  55.3 0.0 collective-permute-done.refs_7_
  55.3 0.6 collective-permute-start.18
  55.8 0.1 collective-permute-start.19
  55.9 0.4 collective-permute-start.20
  56.4 7.7 %evaluate_20.1 = (f32[4,32,128]{2,1,0:T(8,128)S(1)}, f32[4,32,128]{2,1,0:T(8,128)S(1)}) custom-call(s32[1]{0:T(128)} %bitcast.side_ref.refs_0_, s32[1]{0:T(128)} %bitcast.1.refs_1_, bf16[64,128,128]{2,1,0:T(8,128)(2,1)S(1)} %get-tuple-element.22.refs_2_, bf16[64,32,128]{2,1,0:T(8,128)(2,1)S(1)} %get-tuple-element.23.refs_3_, ...), custom_call_target="tpu_custom_call" | custom-call | flops 1677721600 | bytes 4194304 | tf_op jit(solution)/shard_map/evaluate_20/pallas_call | solution.py:30
  64.1 0.1 collective-permute-start.11
  64.2 1.7 %collective-permute-start.7 = (f32[8,32,128]{2,1,0:T(8,128)S(1)}, f32[8,32,128]{2,1,0:T(8,128)S(1)}, u32[]{:S(2)}, u32[]{:S(2)}) collective-permute-start(f32[8,32,128]{2,1,0:T(8,128)S(1)} %add.29.x_ref.refs_11_), channel_id=1, source_target_pairs={{0,2},{2,0},{1,3},{3,1},{4,6},{6,4},{5,7},{7,5},{8,10},{10,8},{9,1... | collective-permute-start | bytes 393224 | tf_op jit(solution)/shard_map/ppermute | solution.py:404
  65.9 1.2 %collective-permute-start.12 = (f32[4,32,128]{2,1,0:T(8,128)S(1)}, f32[4,32,128]{2,1,0:T(8,128)S(1)}, u32[]{:S(2)}, u32[]{:S(2)}) collective-permute-start(f32[4,32,128]{2,1,0:T(8,128)S(1)} %add.33.x_ref.refs_12_), channel_id=1, source_target_pairs={{0,2},{2,0},{1,3},{3,1},{4,6},{6,4},{5,7},{7,5},{8,10},{10,8},{9,1... | collective-permute-start | bytes 196616 | tf_op jit(solution)/shard_map/ppermute | solution.py:404
  67.2 3.4 %collective-permute-done.7.y_ref = f32[8,32,128]{2,1,0:T(8,128)S(1)} collective-permute-done((f32[8,32,128]{2,1,0:T(8,128)S(1)}, f32[8,32,128]{2,1,0:T(8,128)S(1)}, u32[]{:S(2)}, u32[]{:S(2)}) %collective-permute-start.7) | collective-permute-done | bytes 131104 | tf_op jit(solution)/shard_map/ppermute | solution.py:404
  70.5 0.6 collective-permute-start.8
  71.2 0.3 collective-permute-done.12.y_ref
  71.5 1.2 %collective-permute-start.13 = (f32[4,32,128]{2,1,0:T(8,128)S(1)}, f32[4,32,128]{2,1,0:T(8,128)S(1)}, u32[]{:S(2)}, u32[]{:S(2)}) collective-permute-start(f32[4,32,128]{2,1,0:T(8,128)S(1)} %add.34.x_ref), channel_id=1, source_target_pairs={{0,4},{4,0},{8,12},{12,8},{1,5},{5,1},{9,13},{13,9},{2,6},{6,2},{1... | collective-permute-start | bytes 196616 | tf_op jit(solution)/shard_map/ppermute | solution.py:404
  72.7 7.7 %evaluate_24.1 = (f32[2,32,128]{2,1,0:T(8,128)S(1)}, f32[2,32,128]{2,1,0:T(8,128)S(1)}) custom-call(s32[1]{0:T(128)} %bitcast.side_ref.refs_0_, s32[1]{0:T(128)} %bitcast.1.refs_1_, bf16[64,128,128]{2,1,0:T(8,128)(2,1)S(1)} %get-tuple-element.22.refs_2_, bf16[64,32,128]{2,1,0:T(8,128)(2,1)S(1)} %get-tuple-element.23.refs_3_, ...), custom_call_target="tpu_custom_call" | custom-call | flops 1677721600 | bytes 4194304 | tf_op jit(solution)/shard_map/evaluate_24/pallas_call | solution.py:30
  80.4 0.0 copy-start.2
  80.5 7.9 %evaluate_28.1 = (f32[4,32,128]{2,1,0:T(8,128)S(1)}, f32[4,32,128]{2,1,0:T(8,128)S(1)}) custom-call(s32[1]{0:T(128)} %bitcast.side_ref.refs_0_, s32[1]{0:T(128)} %bitcast.1.refs_1_, bf16[64,128,128]{2,1,0:T(8,128)(2,1)S(1)} %get-tuple-element.22.refs_2_, bf16[64,32,128]{2,1,0:T(8,128)(2,1)S(1)} %get-tuple-element.23.refs_3_, ...), custom_call_target="tpu_custom_call" | custom-call | flops 1677721600 | bytes 4194304 | tf_op jit(solution)/shard_map/evaluate_28/pallas_call | solution.py:30
  88.3 0.1 collective-permute-start.16
  88.4 3.3 %collective-permute-start.14 = (f32[4,32,128]{2,1,0:T(8,128)S(1)}, f32[4,32,128]{2,1,0:T(8,128)S(1)}, u32[]{:S(2)}, u32[]{:S(2)}) collective-permute-start(f32[4,32,128]{2,1,0:T(8,128)S(1)} %add.35.x_ref), channel_id=1, source_target_pairs={{0,8},{4,12},{8,0},{12,4},{1,9},{5,13},{9,1},{13,5},{2,10},{6,14},... | collective-permute-start | bytes 196616 | tf_op jit(solution)/shard_map/ppermute | solution.py:404
  91.7 1.1 collective-permute-start.9
  92.9 1.5 %collective-permute-start.17 = (f32[4,32,128]{2,1,0:T(8,128)S(1)}, f32[4,32,128]{2,1,0:T(8,128)S(1)}, u32[]{:S(2)}, u32[]{:S(2)}) collective-permute-start(f32[4,32,128]{2,1,0:T(8,128)S(1)} %add.37.refs_13_.x_ref), channel_id=1, source_target_pairs={{0,2},{2,0},{1,3},{3,1},{4,6},{6,4},{5,7},{7,5},{8,10},{10,8},{9,1... | collective-permute-start | bytes 196616 | tf_op jit(solution)/shard_map/ppermute | solution.py:404
  94.4 1.5 %control_features.1 = (bf16[32,128,32]{2,1,0:T(8,128)(2,1)S(1)}, bf16[32,32,128]{2,1,0:T(8,128)(2,1)S(1)}, bf16[16,128,256]{2,1,0:T(8,128)(2,1)S(1)}, bf16[4,128,256]{2,1,0:T(8,128)(2,1)S(1)}) custom-call(s32[1]{0:T(128)} %bitcast.side_ref.refs_0_, s32[1]{0:T(128)} %bitcast.1.refs_1_, f32[8,128,128]{2,1,0:T(8,128)S(1)} %copy-done.2, ...), custom_call_target="tpu_custom_call" | custom-call | flops 10737418240 | bytes 1048576 | tf_op jit(solution)/shard_map/control_features/pallas_call | solution.py:30
  95.9 1.3 %collective-permute-done.17.y_ref = f32[4,32,128]{2,1,0:T(8,128)S(1)} collective-permute-done((f32[4,32,128]{2,1,0:T(8,128)S(1)}, f32[4,32,128]{2,1,0:T(8,128)S(1)}, u32[]{:S(2)}, u32[]{:S(2)}) %collective-permute-start.17) | collective-permute-done | bytes 65568 | tf_op jit(solution)/shard_map/ppermute | solution.py:404
  97.2 1.2 %collective-permute-start.21 = (f32[4,32,128]{2,1,0:T(8,128)S(1)}, f32[4,32,128]{2,1,0:T(8,128)S(1)}, u32[]{:S(2)}, u32[]{:S(2)}) collective-permute-start(f32[4,32,128]{2,1,0:T(8,128)S(1)} %add.38.refs_0_.x_ref), channel_id=1, source_target_pairs={{0,4},{4,0},{8,12},{12,8},{1,5},{5,1},{9,13},{13,9},{2,6},{6,2},{1... | collective-permute-start | bytes 196616 | tf_op jit(solution)/shard_map/ppermute | solution.py:404
  98.5 4.9 %pairs.1.refs_0_.refs_9_ = bf16[16,512,256]{2,1,0:T(8,128)(2,1)S(1)} custom-call(s32[4,4,8]{2,1,0:T(4,128)S(1)} %convert_dynamic-update-slice_fusion.near_ref.refs_2_, bf16[32,128,32]{2,1,0:T(8,128)(2,1)S(1)} %get-tuple-element.37.left_ref, bf16[32,32,128]{2,1,0:T(8,128)(2,1)S(1)} %get-tuple-element.38.right_ref, f32[4,32,128]{2,1,0:T(8,128)S(1)} %add.38.refs_0_.x_ref), custom_call_target="tpu_custom_call" | custom-call | flops 21474836480 | bytes 1048576 | tf_op jit(solution)/shard_map/pairs/pallas_call | solution.py:30
  103.5 1.9 %collective-permute-start.22 = (f32[4,32,128]{2,1,0:T(8,128)S(1)}, f32[4,32,128]{2,1,0:T(8,128)S(1)}, u32[]{:S(2)}, u32[]{:S(2)}) collective-permute-start(f32[4,32,128]{2,1,0:T(8,128)S(1)} %add.39.x_ref), channel_id=1, source_target_pairs={{0,8},{4,12},{8,0},{12,4},{1,9},{5,13},{9,1},{13,5},{2,10},{6,14},... | collective-permute-start | bytes 196616 | tf_op jit(solution)/shard_map/ppermute | solution.py:404
  105.4 0.6 collective-permute-start.15
  105.9 3.5 %collective-permute-done.22.y_ref = f32[4,32,128]{2,1,0:T(8,128)S(1)} collective-permute-done((f32[4,32,128]{2,1,0:T(8,128)S(1)}, f32[4,32,128]{2,1,0:T(8,128)S(1)}, u32[]{:S(2)}, u32[]{:S(2)}) %collective-permute-start.22) | collective-permute-done | bytes 65568 | tf_op jit(solution)/shard_map/ppermute | solution.py:404
  109.4 0.1 collective-permute-start.23
  109.5 1.2 %collective-permute-done.23.refs_8_ = f32[4,32,128]{2,1,0:T(8,128)S(1)} collective-permute-done((f32[4,32,128]{2,1,0:T(8,128)S(1)}, f32[4,32,128]{2,1,0:T(8,128)S(1)}, u32[]{:S(2)}, u32[]{:S(2)}) %collective-permute-start.23) | collective-permute-done | bytes 65568 | tf_op jit(solution)/shard_map/ppermute | solution.py:404
  110.7 6.1 %solve.1 = (f32[8,32,128]{2,1,0:T(8,128)}, f32[8,32,128]{2,1,0:T(8,128)}) custom-call(s32[1]{0:T(128)} %bitcast.side_ref.refs_0_, s32[1]{0:T(128)} %bitcast.1.refs_1_, s32[4,4,8]{2,1,0:T(4,128)S(1)} %convert_dynamic-update-slice_fusion.near_ref.refs_2_, f32[8,32,128]{2,1,0:T(8,128)S(1)} %add.32.refs_3_, f32[8,32,128]{2,1,0:T(8,128)S(1)} %collective-permute-done.10.refs_4_, ...), custom_call_target="tpu_custom_call" | custom-call | tf_op jit(solution)/shard_map/solve/pallas_call | solution.py:30
  (40 shorter events, 0.2 us)
Async XLA Ops:
  0.6 18.2 %collective-permute-start.3 = (f32[3,8,128]{2,1,0:T(8,128)}, f32[3,8,128]{2,1,0:T(8,128)S(1)}, u32[]{:S(2)}, u32[]{:S(2)}) collective-permute-start(f32[3,8,128]{2,1,0:T(8,128)} %bitcast.26), channel_id=1, source_target_pairs={{0,4},{4,0},{8,12},{12,8},{1,5},{5,1},{9,13},{13,9},{2,6},{6,2},{1... | collective-permute-start | bytes 36872 | tf_op jit(solution)/shard_map/ppermute | solution.py:404
  3.7 15.1 %collective-permute-start.4 = (f32[3,8,128]{2,1,0:T(8,128)}, f32[3,8,128]{2,1,0:T(8,128)S(1)}, u32[]{:S(2)}, u32[]{:S(2)}) collective-permute-start(f32[3,8,128]{2,1,0:T(8,128)} %bitcast.27), channel_id=1, source_target_pairs={{0,8},{4,12},{8,0},{12,4},{1,9},{5,13},{9,1},{13,5},{2,10},{6,14},... | collective-permute-start | bytes 36872 | tf_op jit(solution)/shard_map/ppermute | solution.py:404
  6.3 12.5 %collective-permute-start.5 = (f32[3,8,128]{2,1,0:T(8,128)}, f32[3,8,128]{2,1,0:T(8,128)S(1)}, u32[]{:S(2)}, u32[]{:S(2)}) collective-permute-start(f32[3,8,128]{2,1,0:T(8,128)} %bitcast.28), channel_id=1, source_target_pairs={{0,12},{4,8},{8,4},{12,0},{1,13},{5,9},{9,5},{13,1},{2,14},{6,10},... | collective-permute-start | bytes 36872 | tf_op jit(solution)/shard_map/ppermute | solution.py:404
  6.3 1.0 copy-start
  7.4 1.0 copy-start.1
  8.4 0.9 copy-start.3
  9.3 0.7 copy-start.4
  10.0 0.7 copy-start.5
  10.7 0.7 copy-start.6
  13.7 41.6 %collective-permute-start = (bf16[528,128]{1,0:T(8,128)(2,1)S(1)}, bf16[528,128]{1,0:T(8,128)(2,1)S(1)}, u32[]{:S(2)}, u32[]{:S(2)}) collective-permute-start(bf16[528,128]{1,0:T(8,128)(2,1)S(1)} %get-tuple-element.21), channel_id=1, source_target_pairs={{0,4},{4,0},{8,12},{12,8},{1,5},{5,1},{9,13},{13,9},{2,6},{6,2},{1... | collective-permute-start | bytes 405512 | tf_op jit(solution)/shard_map/ppermute | solution.py:404
  14.6 41.2 %collective-permute-start.1 = (bf16[528,128]{1,0:T(8,128)(2,1)S(1)}, bf16[528,128]{1,0:T(8,128)(2,1)S(1)}, u32[]{:S(2)}, u32[]{:S(2)}) collective-permute-start(bf16[528,128]{1,0:T(8,128)(2,1)S(1)} %get-tuple-element.21), channel_id=1, source_target_pairs={{0,8},{4,12},{8,0},{12,4},{1,9},{5,13},{9,1},{13,5},{2,10},{6,14},... | collective-permute-start | bytes 405512 | tf_op jit(solution)/shard_map/ppermute | solution.py:404
  18.8 37.1 %collective-permute-start.2 = (bf16[528,128]{1,0:T(8,128)(2,1)S(1)}, bf16[528,128]{1,0:T(8,128)(2,1)S(1)}, u32[]{:S(2)}, u32[]{:S(2)}) collective-permute-start(bf16[528,128]{1,0:T(8,128)(2,1)S(1)} %get-tuple-element.21), channel_id=1, source_target_pairs={{0,12},{4,8},{8,4},{12,0},{1,13},{5,9},{9,5},{13,1},{2,14},{6,10},... | collective-permute-start | bytes 405512 | tf_op jit(solution)/shard_map/ppermute | solution.py:404
  47.5 8.9 %collective-permute-start.6 = (f32[8,32,128]{2,1,0:T(8,128)S(1)}, f32[8,32,128]{2,1,0:T(8,128)S(1)}, u32[]{:S(2)}, u32[]{:S(2)}) collective-permute-start(f32[8,32,128]{2,1,0:T(8,128)S(1)} %get-tuple-element.27.refs_9_), channel_id=1, source_target_pairs={{0,1},{1,0},{2,3},{3,2},{4,5},{5,4},{6,7},{7,6},{8,9},{9,8},{10,11... | collective-permute-start | bytes 393224 | tf_op jit(solution)/shard_map/ppermute | solution.py:404
  55.3 37.6 %collective-permute-start.18 = (bf16[528,128]{1,0:T(8,128)(2,1)S(1)}, bf16[528,128]{1,0:T(8,128)(2,1)S(1)}, u32[]{:S(2)}, u32[]{:S(2)}) collective-permute-start(bf16[528,128]{1,0:T(8,128)(2,1)S(1)} %collective-permute-done.refs_7_), channel_id=1, source_target_pairs={{0,1},{1,0},{2,3},{3,2},{4,5},{5,4},{6,7},{7,6},{8,9},{9,8},{10,11... | collective-permute-start | bytes 405512 | tf_op jit(solution)/shard_map/ppermute | solution.py:404
  55.8 38.6 %collective-permute-start.19 = (bf16[528,128]{1,0:T(8,128)(2,1)S(1)}, bf16[528,128]{1,0:T(8,128)(2,1)S(1)}, u32[]{:S(2)}, u32[]{:S(2)}) collective-permute-start(bf16[528,128]{1,0:T(8,128)(2,1)S(1)} %collective-permute-done.1.refs_8_), channel_id=1, source_target_pairs={{0,1},{1,0},{2,3},{3,2},{4,5},{5,4},{6,7},{7,6},{8,9},{9,8},{10,11... | collective-permute-start | bytes 405512 | tf_op jit(solution)/shard_map/ppermute | solution.py:404
  55.9 38.5 %collective-permute-start.20 = (bf16[528,128]{1,0:T(8,128)(2,1)S(1)}, bf16[528,128]{1,0:T(8,128)(2,1)S(1)}, u32[]{:S(2)}, u32[]{:S(2)}) collective-permute-start(bf16[528,128]{1,0:T(8,128)(2,1)S(1)} %collective-permute-done.2.refs_9_), channel_id=1, source_target_pairs={{0,1},{1,0},{2,3},{3,2},{4,5},{5,4},{6,7},{7,6},{8,9},{9,8},{10,11... | collective-permute-start | bytes 405512 | tf_op jit(solution)/shard_map/ppermute | solution.py:404
  64.1 1.8 %collective-permute-start.11 = (f32[4,32,128]{2,1,0:T(8,128)S(1)}, f32[4,32,128]{2,1,0:T(8,128)S(1)}, u32[]{:S(2)}, u32[]{:S(2)}) collective-permute-start(f32[4,32,128]{2,1,0:T(8,128)S(1)} %get-tuple-element.31.refs_10_), channel_id=1, source_target_pairs={{0,1},{1,0},{2,3},{3,2},{4,5},{5,4},{6,7},{7,6},{8,9},{9,8},{10,11... | collective-permute-start | bytes 196616 | tf_op jit(solution)/shard_map/ppermute | solution.py:404
  64.2 6.3 %collective-permute-start.7 = (f32[8,32,128]{2,1,0:T(8,128)S(1)}, f32[8,32,128]{2,1,0:T(8,128)S(1)}, u32[]{:S(2)}, u32[]{:S(2)}) collective-permute-start(f32[8,32,128]{2,1,0:T(8,128)S(1)} %add.29.x_ref.refs_11_), channel_id=1, source_target_pairs={{0,2},{2,0},{1,3},{3,1},{4,6},{6,4},{5,7},{7,5},{8,10},{10,8},{9,1... | collective-permute-start | bytes 393224 | tf_op jit(solution)/shard_map/ppermute | solution.py:404
  65.9 5.5 %collective-permute-start.12 = (f32[4,32,128]{2,1,0:T(8,128)S(1)}, f32[4,32,128]{2,1,0:T(8,128)S(1)}, u32[]{:S(2)}, u32[]{:S(2)}) collective-permute-start(f32[4,32,128]{2,1,0:T(8,128)S(1)} %add.33.x_ref.refs_12_), channel_id=1, source_target_pairs={{0,2},{2,0},{1,3},{3,1},{4,6},{6,4},{5,7},{7,5},{8,10},{10,8},{9,1... | collective-permute-start | bytes 196616 | tf_op jit(solution)/shard_map/ppermute | solution.py:404
  70.5 9.9 %collective-permute-start.8 = (f32[8,32,128]{2,1,0:T(8,128)S(1)}, f32[8,32,128]{2,1,0:T(8,128)S(1)}, u32[]{:S(2)}, u32[]{:S(2)}) collective-permute-start(f32[8,32,128]{2,1,0:T(8,128)S(1)} %add.30.x_ref.refs_9_), channel_id=1, source_target_pairs={{0,4},{4,0},{8,12},{12,8},{1,5},{5,1},{9,13},{13,9},{2,6},{6,2},{1... | collective-permute-start | bytes 393224 | tf_op jit(solution)/shard_map/ppermute | solution.py:404
  71.5 16.9 %collective-permute-start.13 = (f32[4,32,128]{2,1,0:T(8,128)S(1)}, f32[4,32,128]{2,1,0:T(8,128)S(1)}, u32[]{:S(2)}, u32[]{:S(2)}) collective-permute-start(f32[4,32,128]{2,1,0:T(8,128)S(1)} %add.34.x_ref), channel_id=1, source_target_pairs={{0,4},{4,0},{8,12},{12,8},{1,5},{5,1},{9,13},{13,9},{2,6},{6,2},{1... | collective-permute-start | bytes 196616 | tf_op jit(solution)/shard_map/ppermute | solution.py:404
  80.4 14.0 %copy-start.2 = (f32[8,128,128]{2,1,0:T(8,128)S(1)}, f32[8,128,128]{2,1,0:T(8,128)}, u32[]{:S(2)}) copy-start(f32[8,128,128]{2,1,0:T(8,128)} %refs_2_.1) | copy-start | bytes 1572868
  88.3 3.4 %collective-permute-start.16 = (f32[4,32,128]{2,1,0:T(8,128)S(1)}, f32[4,32,128]{2,1,0:T(8,128)S(1)}, u32[]{:S(2)}, u32[]{:S(2)}) collective-permute-start(f32[4,32,128]{2,1,0:T(8,128)S(1)} %get-tuple-element.35), channel_id=1, source_target_pairs={{0,1},{1,0},{2,3},{3,2},{4,5},{5,4},{6,7},{7,6},{8,9},{9,8},{10,11... | collective-permute-start | bytes 196616 | tf_op jit(solution)/shard_map/ppermute | solution.py:404
  88.4 16.9 %collective-permute-start.14 = (f32[4,32,128]{2,1,0:T(8,128)S(1)}, f32[4,32,128]{2,1,0:T(8,128)S(1)}, u32[]{:S(2)}, u32[]{:S(2)}) collective-permute-start(f32[4,32,128]{2,1,0:T(8,128)S(1)} %add.35.x_ref), channel_id=1, source_target_pairs={{0,8},{4,12},{8,0},{12,4},{1,9},{5,13},{9,1},{13,5},{2,10},{6,14},... | collective-permute-start | bytes 196616 | tf_op jit(solution)/shard_map/ppermute | solution.py:404
  91.7 11.7 %collective-permute-start.9 = (f32[8,32,128]{2,1,0:T(8,128)S(1)}, f32[8,32,128]{2,1,0:T(8,128)S(1)}, u32[]{:S(2)}, u32[]{:S(2)}) collective-permute-start(f32[8,32,128]{2,1,0:T(8,128)S(1)} %add.31.x_ref.refs_11_), channel_id=1, source_target_pairs={{0,8},{4,12},{8,0},{12,4},{1,9},{5,13},{9,1},{13,5},{2,10},{6,14},... | collective-permute-start | bytes 393224 | tf_op jit(solution)/shard_map/ppermute | solution.py:404
  92.9 4.3 %collective-permute-start.17 = (f32[4,32,128]{2,1,0:T(8,128)S(1)}, f32[4,32,128]{2,1,0:T(8,128)S(1)}, u32[]{:S(2)}, u32[]{:S(2)}) collective-permute-start(f32[4,32,128]{2,1,0:T(8,128)S(1)} %add.37.refs_13_.x_ref), channel_id=1, source_target_pairs={{0,2},{2,0},{1,3},{3,1},{4,6},{6,4},{5,7},{7,5},{8,10},{10,8},{9,1... | collective-permute-start | bytes 196616 | tf_op jit(solution)/shard_map/ppermute | solution.py:404
  97.2 6.2 %collective-permute-start.21 = (f32[4,32,128]{2,1,0:T(8,128)S(1)}, f32[4,32,128]{2,1,0:T(8,128)S(1)}, u32[]{:S(2)}, u32[]{:S(2)}) collective-permute-start(f32[4,32,128]{2,1,0:T(8,128)S(1)} %add.38.refs_0_.x_ref), channel_id=1, source_target_pairs={{0,4},{4,0},{8,12},{12,8},{1,5},{5,1},{9,13},{13,9},{2,6},{6,2},{1... | collective-permute-start | bytes 196616 | tf_op jit(solution)/shard_map/ppermute | solution.py:404
  103.5 5.9 %collective-permute-start.22 = (f32[4,32,128]{2,1,0:T(8,128)S(1)}, f32[4,32,128]{2,1,0:T(8,128)S(1)}, u32[]{:S(2)}, u32[]{:S(2)}) collective-permute-start(f32[4,32,128]{2,1,0:T(8,128)S(1)} %add.39.x_ref), channel_id=1, source_target_pairs={{0,8},{4,12},{8,0},{12,4},{1,9},{5,13},{9,1},{13,5},{2,10},{6,14},... | collective-permute-start | bytes 196616 | tf_op jit(solution)/shard_map/ppermute | solution.py:404
  105.3 4.2 %collective-permute-start.10 = (f32[8,32,128]{2,1,0:T(8,128)S(1)}, f32[8,32,128]{2,1,0:T(8,128)S(1)}, u32[]{:S(2)}, u32[]{:S(2)}) collective-permute-start(f32[8,32,128]{2,1,0:T(8,128)S(1)} %add.32.refs_3_), channel_id=1, source_target_pairs={{0,1},{1,0},{2,3},{3,2},{4,5},{5,4},{6,7},{7,6},{8,9},{9,8},{10,11... | collective-permute-start | bytes 393224 | tf_op jit(solution)/shard_map/ppermute | solution.py:404
  105.4 4.1 %collective-permute-start.15 = (f32[4,32,128]{2,1,0:T(8,128)S(1)}, f32[4,32,128]{2,1,0:T(8,128)S(1)}, u32[]{:S(2)}, u32[]{:S(2)}) collective-permute-start(f32[4,32,128]{2,1,0:T(8,128)S(1)} %add.36.refs_5_), channel_id=1, source_target_pairs={{0,1},{1,0},{2,3},{3,2},{4,5},{5,4},{6,7},{7,6},{8,9},{9,8},{10,11... | collective-permute-start | bytes 196616 | tf_op jit(solution)/shard_map/ppermute | solution.py:404
  109.4 1.3 %collective-permute-start.23 = (f32[4,32,128]{2,1,0:T(8,128)S(1)}, f32[4,32,128]{2,1,0:T(8,128)S(1)}, u32[]{:S(2)}, u32[]{:S(2)}) collective-permute-start(f32[4,32,128]{2,1,0:T(8,128)S(1)} %add.40.refs_7_), channel_id=1, source_target_pairs={{0,1},{1,0},{2,3},{3,2},{4,5},{5,4},{6,7},{7,6},{8,9},{9,8},{10,11... | collective-permute-start | bytes 196616 | tf_op jit(solution)/shard_map/ppermute | solution.py:404

commit v3 on v2

v3 whole, which is shorter than its diff:
```python
import functools
import math

import jax
import jax.numpy as jnp
from jax import lax
from jax.experimental import pallas as pl
from jax.experimental.pallas import tpu as pltpu
from jax.sharding import PartitionSpec as P

SWEEPS = 2
RADIUS = 1.2
SCALE = 4.0 / RADIUS
GEO = 32
TILE = 4
STEPS = 4
f32, bf16 = jnp.float32, jnp.bfloat16
VMEM = pl.BlockSpec(memory_space=pltpu.VMEM)
SMEM = pl.BlockSpec(memory_space=pltpu.SMEM)
ANY = pl.BlockSpec(memory_space=pl.ANY)
HBM = pl.BlockSpec(memory_space=pltpu.HBM)


def call(kernel, name, out, scratch, operands, specs, cost=None):
    size = 0
    for x in [*out, *scratch, *operands]:
        if len(x.shape) < 2:
            continue
        size += math.prod(x.shape[:-1]) * max(x.shape[-1], 128) * jnp.dtype(x.dtype).itemsize
    return pl.pallas_call(
        kernel,
        out_shape=out,
        in_specs=specs,
        out_specs=[VMEM] * len(out),
        scratch_shapes=scratch,
        compiler_params=pltpu.CompilerParams(vmem_limit_bytes=size + (4 << 20)),
        cost_estimate=cost,
        name=name,
    )(*operands)


def shape(dims, kind):
    return jax.ShapeDtypeStruct(dims, kind)


def root_of(square):
    root = jnp.maximum(square, 1e-12)
    return root * lax.rsqrt(root)


def split3(v):
    a = v.astype(bf16).astype(f32)
    b = (v - a).astype(bf16).astype(f32)
    return (a, b, v - a - b)


def pairs_of_parts():
    return [(a, b) for a in range(3) for b in range(3) if a + b < 4]


def left_rows(xyz):
    rows = []
    for v in xyz:
        parts = split3(v)
        rows += [parts[a] for a, b in pairs_of_parts()]
    rows += list(split3(sum(v * v for v in xyz)))
    return rows + [jnp.ones_like(xyz[0])] * 3


def right_rows(xyz):
    rows = []
    for v in xyz:
        parts = split3(v)
        rows += [-2.0 * parts[b] for a, b in pairs_of_parts()]
    rows += [jnp.ones_like(xyz[0])] * 3
    return rows + list(split3(sum(v * v for v in xyz)))


def told(ref, count):
    rows = ref[ref.shape[0] - 10 * count :].astype(f32)
    part = [rows[n * count : (n + 1) * count] for n in range(10)]
    xyz = [((part[3 * d + 2] + part[3 * d + 1]) + part[3 * d]) * SCALE for d in range(3)]
    return xyz, part[9]


def fill_rows(scratch, rows):
    for g, row in enumerate(rows):
        scratch[:, g, :] = row
    for g in range(len(rows), scratch.shape[1]):
        scratch[:, g, :] = jnp.zeros_like(rows[0])


def prepare_kernel(
    side_ref, volume_hbm, listed_hbm, grad_hbm, control_hbm, inverse_hbm, near_hbm, *refs
):
    left_ref, counts_ref, grad_ref, parcel_ref = refs[:4]
    coords, listed, scratch, tally, inverse, control, near, sems = refs[4:]
    half = inverse.shape[0]
    own = 2 * half
    mine = pl.ds(side_ref[0] * half, half)
    copies = [
        pltpu.make_async_copy(source, target, sems.at[n])
        for n, (source, target) in enumerate(
            [
                (volume_hbm, coords),
                (listed_hbm, listed),
                (inverse_hbm.at[mine], inverse),
                (near_hbm, near),
                (control_hbm, control),
                (grad_hbm, grad_ref),
            ]
        )
    ]
    for copy in copies:
        copy.start()
    copies[0].wait()
    fill_rows(scratch, left_rows([coords[d] * SCALE for d in range(3)]))
    blocks, width, depth = left_ref.shape
    lane = lax.broadcasted_iota(jnp.int32, (width, depth), 1)

    def one(s, _):
        turned = scratch[s].T
        turned = jnp.concatenate([turned, jnp.zeros((width, depth - GEO), f32)], axis=1)
        left_ref[s] = jnp.where(lane == s + GEO, 1.0, turned).astype(bf16)
        return 0

    lax.fori_loop(0, blocks, one, 0, unroll=8)
    copies[1].wait()
    chosen = listed[...]
    nodes = counts_ref.shape[0]
    tally[...] = jnp.zeros_like(tally)
    for c in range(nodes * own):
        tally[c : c + 1, 0:blocks] = jnp.sum(
            jnp.where(chosen == c, 1.0, 0.0), axis=0, keepdims=True
        )
    for n in range(nodes):
        turned = tally[n * own : (n + 1) * own, :].T[0:blocks]
        counts_ref[n] = jnp.concatenate([turned, jnp.zeros((blocks, width - own), f32)], axis=1)
    for copy in copies[2:]:
        copy.wait()
    for q in range(half):
        parcel_ref[q * 128 : (q + 1) * 128] = inverse[q].astype(bf16)
    rows = [part for d in range(3) for part in split3(control[d])]
    numbers = near[...].astype(f32)
    numbers = jnp.concatenate([numbers, jnp.zeros((near.shape[0], width - own), f32)], axis=1)
    rows.append(jnp.concatenate([numbers, jnp.zeros((own - near.shape[0], width), f32)], axis=0))
    parcel_ref[half * 128 :] = jnp.concatenate(rows, axis=0).astype(bf16)


def chunk_kernel(step, listed, *refs):
    side_ref, me_ref, left_ref, grad_ref, counts_ref, parcel_ref = refs[:6]
    keep_ref, send_ref, features, rhs, total, result, d0, d1, p0, p1 = refs[-10:]
    blocks = grad_ref.shape[0]
    per = features.shape[0]
    depth = rhs.shape[1]
    steps = blocks // TILE
    pairs = per // 2
    whole = pairs * steps
    size = TILE * 128
    counts = counts_ref[me_ref[0] ^ step][:, 0:per].astype(jnp.int32)
    most = jnp.max(counts)
    layers = jnp.int32(0)
    for b in range(listed.bit_length()):
        layers = layers + jnp.where(most >= (1 << b), 1, 0)
    result[...] = jnp.zeros_like(result)
    fill_rows(features, right_rows(told(parcel_ref, per)[0]))
    rhs[...] = jnp.zeros_like(rhs)
    for c in range(per):
        rhs[c // 2, 0:GEO, (c % 2) * 128 : (c % 2 + 1) * 128] = features[c].astype(bf16)

    def distances(t, d):
        j, i = t // steps, t % steps
        left = left_ref[pl.ds(i * TILE, TILE)].reshape(size, depth)
        d[...] = jnp.dot(left, rhs[j], preferred_element_type=f32)

    def values(d, p):
        root = root_of(d[...])
        inside = jnp.maximum(4.0 - root, 0.0)
        twice = inside * inside
        p[0:size] = (twice * twice).astype(bf16)
        p[size:] = root.astype(bf16)

    def products(t, p):
        j, i = t // steps, t % steps
        g = jnp.concatenate([grad_ref[i * TILE + q] for q in range(TILE)], axis=1)
        even, odd = p[0:size], p[0:size] * p[size:]
        total[j] += (
            jnp.dot(g, even, preferred_element_type=f32)
            + jnp.dot(g, odd, preferred_element_type=f32)
        )

    def layer(b, weight):
        for c in range(per):
            bit = jnp.bitwise_and(lax.shift_right_logical(counts[:, c : c + 1], b), 1)
            far = jnp.where(jnp.broadcast_to(bit, (blocks, 128)) == 1, 0.0, 65536.0)
            rhs[c // 2, GEO : GEO + blocks, (c % 2) * 128 : (c % 2 + 1) * 128] = far.astype(bf16)
        total[...] = jnp.zeros_like(total)
        p1[...] = jnp.zeros_like(p1)
        distances(0, d0)

        def turn(h, _):
            for u in range(STEPS):
                t = STEPS * h + u
                d, p = (d0, p0) if u % 2 == 0 else (d1, p1)
                later, done = (d1, p1) if u % 2 == 0 else (d0, p0)
                values(d, p)
                products(jnp.maximum(t - 1, 0), done)
                distances(jnp.minimum(t + 1, whole - 1), later)
            return 0

        lax.fori_loop(0, whole // STEPS, turn, 0)
        products(whole - 1, p1)
        result[...] += weight * total[...]
        return weight * 2.0

    lax.fori_loop(0, layers, layer, jnp.float32(1.0 / 256.0))
    side = side_ref[0]
    half = pairs // 2
    for j in range(half):
        mine = result[side * half + j]
        other = result[(1 - side) * half + j]
        for q in range(2):
            keep_ref[2 * j + q] = mine[:, q * 128 : (q + 1) * 128]
            send_ref[2 * j + q] = other[:, q * 128 : (q + 1) * 128]


def features_kernel(nodes, side_ref, me_ref, inverse_hbm, *refs):
    parcels = refs[:nodes]
    others = refs[nodes : 2 * nodes - 1]
    left_ref, right_ref, high_ref, low_ref, near_ref, coords, features, inverse, sem = refs[-9:]
    copy = pltpu.make_async_copy(inverse_hbm, inverse, sem.at[0])
    copy.start()
    own = inverse.shape[0]
    half = own // 2
    side, me = side_ref[0], me_ref[0]
    for step in range(nodes):
        xyz, numbers = told(parcels[step], own)
        for d in range(3):
            coords[d, me ^ step] = xyz[d]
        near_ref[me ^ step] = numbers.astype(jnp.int32)
    for step in range(1, nodes):
        for core, parcel in ((side, parcels[step]), (1 - side, others[step - 1])):
            for c in range(half):
                pair = (me ^ step) * half + core * (half // 2) + c // 2
                at = (c % 2) * 128
                high_ref[pair, :, at : at + 128] = parcel[c * 128 : (c + 1) * 128]
    blocks = left_ref.shape[0]
    xyz = [coords[d].reshape(blocks, 128) for d in range(3)]
    fill_rows(features, right_rows(xyz))
    right_ref[...] = features[...].astype(bf16)
    fill_rows(features, left_rows(xyz))

    def turn_left(c, _):
        left_ref[c] = features[c].T.astype(bf16)
        return 0

    lax.fori_loop(0, blocks, turn_left, 0, unroll=8)
    copy.wait()
    for c in range(own):
        inv = inverse[c]
        high = inv.astype(bf16)
        at = (c % 2) * 128
        high_ref[me * half + c // 2, :, at : at + 128] = high
        low_ref[c // 2, :, at : at + 128] = (inv - high.astype(f32)).astype(bf16)


def pairs_kernel(near_ref, left_ref, right_ref, *refs):
    phi_ref, d0, d1 = refs[-3:]
    blocks = right_ref.shape[0]
    own = near_ref.shape[1]
    coupled = phi_ref.shape[1] // 128

    def distances(c, d):
        points = [left_ref[near_ref[c // own, k, c % own]] for k in range(coupled)]
        d[...] = jnp.dot(jnp.concatenate(points, axis=0), right_ref[c], preferred_element_type=f32)

    def values(pair, q, d):
        root = root_of(d[...])
        inside = jnp.maximum(1.0 - 0.25 * root, 0.0)
        twice = inside * inside
        phi_ref[pair, :, q * 128 : (q + 1) * 128] = ((twice * twice) * (1.0 + root)).astype(bf16)

    distances(0, d0)

    def turn(h, _):
        for u in range(STEPS):
            c = STEPS * h + u
            values(2 * h + u // 2, u % 2, d0 if u % 2 == 0 else d1)
            distances(jnp.minimum(c + 1, blocks - 1), d1 if u % 2 == 0 else d0)
        return 0

    lax.fori_loop(0, blocks // STEPS, turn, 0)


def add_kernel(x_ref, y_ref, *refs):
    refs[-1][...] = x_ref[...] + y_ref[...]


def finish_kernel(x_ref, y_ref, *refs):
    both = x_ref[...] + y_ref[...]
    refs[-2][...] = both
    refs[-1][...] = both.astype(bf16)


def solve_kernel(nodes, side_ref, me_ref, near_ref, *refs):
    mine, theirs = refs[:nodes], refs[nodes : 2 * nodes]
    phi_ref, high_ref, low_ref, grad_out, adjoint_out, grads, values0, values1 = refs[2 * nodes :]
    pairs = high_ref.shape[0]
    own = near_ref.shape[1]
    coupled = phi_ref.shape[1] // 128
    side, me = side_ref[0], me_ref[0]
    half = own // 2
    for step in range(nodes):
        at = (me ^ step) * own
        grads[pl.ds(at + side * half, half)] = mine[step][...].astype(f32)
        grads[pl.ds(at + (1 - side) * half, half)] = theirs[step][...].astype(f32)

    def through(two, weights, exact):
        rows = []
        for x in two:
            high = x.astype(bf16)
            low = (x - high.astype(f32)).astype(bf16)
            rows.append(jnp.concatenate([high, high], axis=1) if exact else high)
            rows.append(jnp.concatenate([low, jnp.zeros_like(low)], axis=1) if exact else low)
        out = jnp.dot(jnp.concatenate(rows, axis=0), weights, preferred_element_type=f32)
        n = two[0].shape[0]
        return [
            out[2 * q * n : (2 * q + 1) * n, q * 128 : (q + 1) * 128]
            + out[(2 * q + 1) * n : (2 * q + 2) * n, q * 128 : (q + 1) * 128]
            for q in range(2)
        ]

    def start(pair, _):
        done = through([grads[2 * pair], grads[2 * pair + 1]], high_ref[pair], False)
        for q in range(2):
            values0[2 * pair + q] = done[q].astype(bf16)
        return 0

    lax.fori_loop(0, pairs, start, 0, unroll=8)

    def rest(old, pair):
        near = []
        for q in range(2):
            c = 2 * pair + q
            near.append(
                jnp.concatenate(
                    [old[near_ref[c // own, k, c % own]] for k in range(coupled)], axis=1
                )
            )
        n = near[0].shape[0]
        coupling = jnp.dot(
            jnp.concatenate(near, axis=0), phi_ref[pair], preferred_element_type=f32
        )
        return [
            grads[2 * pair + q] - coupling[q * n : (q + 1) * n, q * 128 : (q + 1) * 128]
            for q in range(2)
        ]

    old, new = values0, values1
    for sweep in range(SWEEPS - 1):
        def one(pair, _, old=old, new=new):
            done = through(rest(old, pair), high_ref[pair], False)
            for q in range(2):
                new[2 * pair + q] = done[q].astype(bf16)
            return 0

        lax.fori_loop(0, pairs, one, 0, unroll=8)
        old, new = new, old

    first = me * half
    for pair in range(own // 2):
        weights = jnp.concatenate([high_ref[first + pair], low_ref[pair]], axis=0)
        done = through(rest(old, first + pair), weights, True)
        for q in range(2):
            grad_out[2 * pair + q] = grads[2 * (first + pair) + q]
            adjoint_out[2 * pair + q] = done[q]


def exchange(x, axis, size, step):
    return lax.ppermute(x, axis, [(i, i ^ step) for i in range(size)])


def doubling(size):
    return [1 << b for b in range(size.bit_length() - 1)]


def local(sizes, volume_grad, volume_coords, support, control_coords, neighbours, block_inverse):
    nodes, fns, subs = sizes["node"], sizes["fn"], sizes["sub"]
    blocks, funcs, width = volume_grad.shape
    own, coupled = neighbours.shape
    controls = own * nodes
    depth = -(-(blocks + GEO) // 128) * 128
    side = lax.axis_index("sub").astype(jnp.int32).reshape(1)
    me = lax.axis_index("node").astype(jnp.int32).reshape(1)

    def hbm(x):
        return pltpu.with_memory_space_constraint(x, pltpu.HBM)

    operands = [
        hbm(x)
        for x in (
            volume_coords.transpose(1, 0, 2),
            support.T,
            volume_grad,
            control_coords.transpose(1, 0, 2),
            block_inverse,
            neighbours.T,
        )
    ]
    half = own // 2
    left, counts, grads, parcel = call(
        prepare_kernel,
        "prepare",
        [
            shape((blocks, width, depth), bf16),
            shape((nodes, blocks, width), f32),
            shape(volume_grad.shape, volume_grad.dtype),
            shape((half * width + 10 * own, width), bf16),
        ],
        [
            pltpu.VMEM((3, blocks, width), f32),
            pltpu.VMEM(support.T.shape, jnp.int32),
            pltpu.VMEM((blocks, GEO, width), f32),
            pltpu.VMEM((controls, width), f32),
            pltpu.VMEM((half, width, width), f32),
            pltpu.VMEM((3, own, width), f32),
            pltpu.VMEM((coupled, own), jnp.int32),
            pltpu.SemaphoreType.DMA((6,)),
        ],
        [side, *operands],
        [SMEM] + [HBM] * 6,
    )
    parcels = [parcel] + [exchange(parcel, "node", nodes, step) for step in range(1, nodes)]

    def evaluate(step, after):
        entries = blocks * own * width * width
        operands = [side, me, left, grads, counts, parcels[step]]
        return call(
            functools.partial(chunk_kernel, step, support.shape[1]),
            f"evaluate_{step}",
            [shape((half, funcs, width), f32)] * 2,
            [
                pltpu.VMEM((own, GEO, width), f32),
                pltpu.VMEM((half, depth, 2 * width), bf16),
                pltpu.VMEM((half, funcs, 2 * width), f32),
                pltpu.VMEM((half, funcs, 2 * width), f32),
                pltpu.VMEM((TILE * width, 2 * width), f32),
                pltpu.VMEM((TILE * width, 2 * width), f32),
                pltpu.VMEM((2 * TILE * width, 2 * width), bf16),
                pltpu.VMEM((2 * TILE * width, 2 * width), bf16),
            ],
            operands + after,
            [SMEM, SMEM] + [VMEM] * 4 + [ANY] * len(after),
            pl.CostEstimate(flops=entries * 400, bytes_accessed=4 << 20, transcendentals=entries),
        )

    def add(x, y, after=(), kernel=add_kernel, name="add", kinds=(f32,)):
        done = call(
            kernel,
            name,
            [shape(x.shape, kind) for kind in kinds],
            [],
            [x, y, *after],
            [VMEM, VMEM] + [ANY] * len(after),
        )
        return done if len(done) > 1 else done[0]

    keep, send = evaluate(0, [])
    last = send
    held = None
    arrived = None
    hold = []
    for step in range(nodes - 1, 0, -1):
        mine, other = evaluate(step, [last] + hold)
        if held is None:
            held = add(keep, exchange(send, "sub", subs, 1), [other])
        else:
            held = add(held, arrived, [other])
        part = add(mine, exchange(other, "sub", subs, 1))
        arrived = exchange(part, "node", nodes, step)
        last, hold = other, [part]

    others = [exchange(x, "sub", subs, 1) for x in parcels[1:]]
    operands = [side, me, hbm(block_inverse), *parcels, *others]
    control_left, control_right, high, low, near = call(
        functools.partial(features_kernel, nodes),
        "control_features",
        [
            shape((controls, width, GEO), bf16),
            shape((controls, GEO, width), bf16),
            shape((controls // 2, width, 2 * width), bf16),
            shape((half, width, 2 * width), bf16),
            shape((nodes, own, width), jnp.int32),
        ],
        [
            pltpu.VMEM((3, nodes, own, width), f32),
            pltpu.VMEM((controls, GEO, width), f32),
            pltpu.VMEM((own, width, width), f32),
            pltpu.SemaphoreType.DMA((1,)),
        ],
        operands + hold,
        [SMEM, SMEM, HBM] + [VMEM] * (2 * nodes - 1) + [ANY],
        pl.CostEstimate(flops=10 << 30, bytes_accessed=1 << 20, transcendentals=0),
    )
    held = add(held, arrived, [high])
    (phi,) = call(
        pairs_kernel,
        "pairs",
        [shape((controls // 2, coupled * width, 2 * width), bf16)],
        [
            pltpu.VMEM((coupled * width, width), f32),
            pltpu.VMEM((coupled * width, width), f32),
        ],
        [near, control_left, control_right, held],
        [SMEM, VMEM, VMEM, ANY],
        pl.CostEstimate(flops=20 << 30, bytes_accessed=1 << 20, transcendentals=2 << 20),
    )
    *steps, final = doubling(fns)
    for step in steps:
        held = add(held, exchange(held, "fn", fns, step))
    held, rounded = add(
        held, exchange(held, "fn", fns, final), [phi], finish_kernel, "finish", (f32, bf16)
    )
    mine = [held] + [exchange(rounded, "node", nodes, step) for step in range(1, nodes)]
    theirs = [exchange(x, "sub", subs, 1) for x in mine]
    return tuple(
        call(
            functools.partial(solve_kernel, nodes),
            "solve",
            [shape((own, funcs, width), f32)] * 2,
            [
                pltpu.VMEM((controls, funcs, width), f32),
                pltpu.VMEM((controls, funcs, width), bf16),
                pltpu.VMEM((controls, funcs, width), bf16),
            ],
            [side, me, near, *mine, *theirs, phi, high, low],
            [SMEM, SMEM, SMEM] + [VMEM] * (2 * nodes + 3),
        )
    )


def solution(mesh):
    return jax.shard_map(
        functools.partial(local, dict(mesh.shape)),
        mesh=mesh,
        in_specs=(
            P(("sect", "node", "fn", "sub"), None, None),
            P(("sect", "node", "fn", "sub"), None, None),
            P(("sect", "node", "fn", "sub"), None),
            P(("sect", "node"), None, None),
            P(("sect", "node"), None),
            P(("sect", "node"), None, None),
        ),
        out_specs=(P(("sect", "node"), None, None), P(("sect", "node"), None, None)),
        check_vma=False,
    )
```

time: 117 us -> 101 us (0.86)
  starting transfers between devices: 25.9 us -> 17.1 us
  local copies, waits for them, and re-layouts: 5.78 us -> 0 us
    ppermute x24 -> x21, starting transfers between devices: 25.9 us -> 17.1 us  [exchange(): return lax.ppermute(x, axis, [(i, i ^ step) for i in range(size)])]
    unnamed x14 -> x0, local copies, waits for them, and re-layouts: 5.09 us -> none
    pallas_call x21 -> x16, Pallas kernels: 74.5 us -> 73.4 us  [call(): pl.pallas_call(kernel, out_shape=out, in_specs=specs, out_specs=[VMEM] *...]
    ppermute x24 -> x21, waiting for transfers between devices: 9.7 us -> 9.34 us  [exchange(): return lax.ppermute(x, axis, [(i, i ^ step) for i in range(size)])]
  transfers between devices with their start and end apart: 24 -> 21, of which waited for: 5 -> 8; matrix products, arithmetic and copies ran while one was open for 1% -> 0% of each run, Pallas kernels for 59% -> 64%
where the time goes in v3:
time: 101 us
  Pallas kernels  73.4 us (73%)
  starting transfers between devices  17.1 us (17%)
  waiting for transfers between devices  9.34 us (9%)
    pallas_call x16, Pallas kernels, call(): pl.pallas_call(kernel, out_shape=out, in_specs=specs, out_specs=[VMEM] *...  73.4 us
    ppermute x21, starting transfers between devices, exchange(): return lax.ppermute(x, axis, [(i, i ^ step) for i in range(size)])  17.1 us
    ppermute x21, waiting for transfers between devices, exchange(): return lax.ppermute(x, axis, [(i, i ^ step) for i in range(size)])  9.34 us
  transfers between devices with their start and end apart: 21, of which 8 were waited for; matrix products, arithmetic and copies ran while one was open for 0% of the time, Pallas kernels for 64%

profile of v3, /device:TPU:0, one launch (start us, length us, event | category | flops | bytes accessed | tf_op | source)
XLA Modules:
  0.0 100.6 jit_solution(7707358740926125737)
XLA Ops:
  0.6 3.0 %prepare.1 = (bf16[64,128,128]{2,1,0:T(8,128)(2,1)S(1)}, f32[4,64,128]{2,1,0:T(8,128)S(1)}, bf16[64,32,128]{2,1,0:T(8,128)(2,1)S(1)}, bf16[592,128]{1,0:T(8,128)(2,1)S(1)}) custom-call(s32[1]{0:T(128)} %bitcast.side_ref.refs_0_, f32[3,64,128]{2,1,0:T(8,128)} %bitcast.6, s32[32,64]{1,0:T(8,128)} %bitcast.7, bf16[64,32,128]{2,1,0:T(8,128)(2,1)} %grad_hbm.1, ...), custom_call_target="tpu_custom_call" | custom-call | tf_op jit(solution)/shard_map/prepare/pallas_call | solution.py:30
  3.6 5.1 %collective-permute-start.2 = (bf16[592,128]{1,0:T(8,128)(2,1)S(1)}, bf16[592,128]{1,0:T(8,128)(2,1)S(1)}, u32[]{:S(2)}, u32[]{:S(2)}) collective-permute-start(bf16[592,128]{1,0:T(8,128)(2,1)S(1)} %get-tuple-element.21.refs_5_.refs_0_), channel_id=1, source_target_pairs={{0,12},{4,8},{8,4},{12,0},{1,13},{5,9},{9,5},{13,1},{2,14},{6,10},... | collective-permute-start | bytes 454664 | tf_op jit(solution)/shard_map/ppermute | solution.py:380
  8.7 0.0 collective-permute-start.1
  8.7 14.4 %evaluate_0.1 = (f32[4,32,128]{2,1,0:T(8,128)S(1)}, f32[4,32,128]{2,1,0:T(8,128)S(1)}) custom-call(s32[1]{0:T(128)} %bitcast.side_ref.refs_0_, s32[1]{0:T(128)} %bitcast.1.refs_1_.me_ref, bf16[64,128,128]{2,1,0:T(8,128)(2,1)S(1)} %get-tuple-element.22.refs_2_, bf16[64,32,128]{2,1,0:T(8,128)(2,1)S(1)} %get-tuple-element.23.refs_3_, ...), custom_call_target="tpu_custom_call" | custom-call | flops 3355443200 | bytes 4194304 | tf_op jit(solution)/shard_map/evaluate_0/pallas_call | solution.py:30
  23.1 0.0 collective-permute-done.2.refs_5_.refs_3_
  23.1 14.4 %evaluate_3.1 = (f32[4,32,128]{2,1,0:T(8,128)S(1)}, f32[4,32,128]{2,1,0:T(8,128)S(1)}) custom-call(s32[1]{0:T(128)} %bitcast.side_ref.refs_0_, s32[1]{0:T(128)} %bitcast.1.refs_1_.me_ref, bf16[64,128,128]{2,1,0:T(8,128)(2,1)S(1)} %get-tuple-element.22.refs_2_, bf16[64,32,128]{2,1,0:T(8,128)(2,1)S(1)} %get-tuple-element.23.refs_3_, ...), custom_call_target="tpu_custom_call" | custom-call | flops 3355443200 | bytes 4194304 | tf_op jit(solution)/shard_map/evaluate_3/pallas_call | solution.py:30
  37.5 0.1 collective-permute-start.6
  37.6 0.7 collective-permute-start
  38.3 0.5 collective-permute-done.6.y_ref
  38.8 0.0 collective-permute-done.1.refs_5_.refs_2_
  38.8 14.4 %evaluate_2.1 = (f32[4,32,128]{2,1,0:T(8,128)S(1)}, f32[4,32,128]{2,1,0:T(8,128)S(1)}) custom-call(s32[1]{0:T(128)} %bitcast.side_ref.refs_0_, s32[1]{0:T(128)} %bitcast.1.refs_1_.me_ref, bf16[64,128,128]{2,1,0:T(8,128)(2,1)S(1)} %get-tuple-element.22.refs_2_, bf16[64,32,128]{2,1,0:T(8,128)(2,1)S(1)} %get-tuple-element.23.refs_3_, ...), custom_call_target="tpu_custom_call" | custom-call | flops 3355443200 | bytes 4194304 | tf_op jit(solution)/shard_map/evaluate_2/pallas_call | solution.py:30
  53.2 0.2 collective-permute-start.7
  53.4 0.4 collective-permute-start.9
  53.8 0.2 collective-permute-start.4
  54.0 0.4 collective-permute-start.5
  54.3 0.0 collective-permute-done.refs_5_.refs_1_
  54.3 0.2 collective-permute-start.3
  54.5 0.1 collective-permute-done.7.y_ref
  54.5 3.2 %collective-permute-start.10 = (f32[4,32,128]{2,1,0:T(8,128)S(1)}, f32[4,32,128]{2,1,0:T(8,128)S(1)}, u32[]{:S(2)}, u32[]{:S(2)}) collective-permute-start(f32[4,32,128]{2,1,0:T(8,128)S(1)} %add.7.refs_7_), channel_id=1, source_target_pairs={{0,12},{4,8},{8,4},{12,0},{1,13},{5,9},{9,5},{13,1},{2,14},{6,10},... | collective-permute-start | bytes 196616 | tf_op jit(solution)/shard_map/ppermute | solution.py:380
  57.8 14.4 %evaluate_1.1 = (f32[4,32,128]{2,1,0:T(8,128)S(1)}, f32[4,32,128]{2,1,0:T(8,128)S(1)}) custom-call(s32[1]{0:T(128)} %bitcast.side_ref.refs_0_, s32[1]{0:T(128)} %bitcast.1.refs_1_.me_ref, bf16[64,128,128]{2,1,0:T(8,128)(2,1)S(1)} %get-tuple-element.22.refs_2_, bf16[64,32,128]{2,1,0:T(8,128)(2,1)S(1)} %get-tuple-element.23.refs_3_, ...), custom_call_target="tpu_custom_call" | custom-call | flops 3355443200 | bytes 4194304 | tf_op jit(solution)/shard_map/evaluate_1/pallas_call | solution.py:30
  72.1 0.0 collective-permute-done.9.y_ref
  72.2 0.1 collective-permute-start.8
  72.3 0.0 collective-permute-done.10.y_ref
  72.3 0.1 collective-permute-start.11
  72.4 1.1 %collective-permute-done.8.y_ref = f32[4,32,128]{2,1,0:T(8,128)S(1)} collective-permute-done((f32[4,32,128]{2,1,0:T(8,128)S(1)}, f32[4,32,128]{2,1,0:T(8,128)S(1)}, u32[]{:S(2)}, u32[]{:S(2)}) %collective-permute-start.8) | collective-permute-done | bytes 65568 | tf_op jit(solution)/shard_map/ppermute | solution.py:380
  73.5 0.3 collective-permute-start.12
  73.8 0.0 collective-permute-done.3.refs_4_
  73.8 0.0 collective-permute-done.4.refs_5_
  73.8 0.0 collective-permute-done.5.refs_6_
  73.8 1.5 %control_features.1 = (bf16[32,128,32]{2,1,0:T(8,128)(2,1)S(1)}, bf16[32,32,128]{2,1,0:T(8,128)(2,1)S(1)}, bf16[16,128,256]{2,1,0:T(8,128)(2,1)S(1)}, bf16[4,128,256]{2,1,0:T(8,128)(2,1)S(1)}, s32[4,8,128]{2,1,0:T(8,128)S(1)}) custom-call(s32[1]{0:T(128)} %bitcast.side_ref.refs_0_, s32[1]{0:T(128)} %bitcast.1.refs_1_.me_ref, f32[8,128,128]{2,1,0:T(8,128)} %inverse_hbm.3, ...), custom_call_target="tpu_custom_call" | custom-call | flops 10737418240 | bytes 1048576 | tf_op jit(solution)/shard_map/control_features/pallas_call | solution.py:30
  75.3 3.6 %collective-permute-done.11.y_ref = f32[4,32,128]{2,1,0:T(8,128)S(1)} collective-permute-done((f32[4,32,128]{2,1,0:T(8,128)S(1)}, f32[4,32,128]{2,1,0:T(8,128)S(1)}, u32[]{:S(2)}, u32[]{:S(2)}) %collective-permute-start.11) | collective-permute-done | bytes 65568 | tf_op jit(solution)/shard_map/ppermute | solution.py:380
  79.0 0.2 collective-permute-done.12.y_ref
  79.2 1.6 %collective-permute-start.13 = (f32[4,32,128]{2,1,0:T(8,128)S(1)}, f32[4,32,128]{2,1,0:T(8,128)S(1)}, u32[]{:S(2)}, u32[]{:S(2)}) collective-permute-start(f32[4,32,128]{2,1,0:T(8,128)S(1)} %add.13.refs_0_.x_ref), channel_id=1, source_target_pairs={{0,2},{2,0},{1,3},{3,1},{4,6},{6,4},{5,7},{7,5},{8,10},{10,8},{9,1... | collective-permute-start | bytes 196616 | tf_op jit(solution)/shard_map/ppermute | solution.py:380
  80.7 5.1 %pairs.1.refs_0_.refs_8_ = bf16[16,512,256]{2,1,0:T(8,128)(2,1)S(1)} custom-call(s32[4,8,128]{2,1,0:T(8,128)S(1)} %get-tuple-element.32.near_ref, bf16[32,128,32]{2,1,0:T(8,128)(2,1)S(1)} %get-tuple-element.35.left_ref, bf16[32,32,128]{2,1,0:T(8,128)(2,1)S(1)} %get-tuple-element.36.right_ref, f32[4,32,128]{2,1,0:T(8,128)S(1)} %add.13.refs_0_.x_ref), custom_call_target="tpu_custom_call" | custom-call | flops 21474836480 | bytes 1048576 | tf_op jit(solution)/shard_map/pairs/pallas_call | solution.py:30
  85.8 0.0 collective-permute-done.13.y_ref
  85.9 0.1 collective-permute-start.14
  85.9 1.5 %collective-permute-start.15 = (bf16[4,32,128]{2,1,0:T(8,128)(2,1)S(1)}, bf16[4,32,128]{2,1,0:T(8,128)(2,1)S(1)}, u32[]{:S(2)}, u32[]{:S(2)}) collective-permute-start(bf16[4,32,128]{2,1,0:T(8,128)(2,1)S(1)} %get-tuple-element.38), channel_id=1, source_target_pairs={{0,8},{4,12},{8,0},{12,4},{1,9},{5,13},{9,1},{13,5},{2,10},{6,14},... | collective-permute-start | bytes 98312 | tf_op jit(solution)/shard_map/ppermute | solution.py:380
  87.4 0.0 collective-permute-start.17
  87.4 2.9 %collective-permute-start.16 = (bf16[4,32,128]{2,1,0:T(8,128)(2,1)S(1)}, bf16[4,32,128]{2,1,0:T(8,128)(2,1)S(1)}, u32[]{:S(2)}, u32[]{:S(2)}) collective-permute-start(bf16[4,32,128]{2,1,0:T(8,128)(2,1)S(1)} %get-tuple-element.38), channel_id=1, source_target_pairs={{0,12},{4,8},{8,4},{12,0},{1,13},{5,9},{9,5},{13,1},{2,14},{6,10},... | collective-permute-start | bytes 98312 | tf_op jit(solution)/shard_map/ppermute | solution.py:380
  90.3 0.0 collective-permute-done.14.refs_1_
  90.3 0.2 collective-permute-start.18
  90.5 0.3 collective-permute-done.15.refs_2_
  90.8 0.0 collective-permute-start.19
  90.9 2.3 %collective-permute-done.16.refs_3_ = bf16[4,32,128]{2,1,0:T(8,128)(2,1)S(1)} collective-permute-done((bf16[4,32,128]{2,1,0:T(8,128)(2,1)S(1)}, bf16[4,32,128]{2,1,0:T(8,128)(2,1)S(1)}, u32[]{:S(2)}, u32[]{:S(2)}) %collective-permute-start.16) | collective-permute-done | bytes 32800 | tf_op jit(solution)/shard_map/ppermute | solution.py:380
  93.1 0.0 collective-permute-start.20
  93.1 0.0 collective-permute-done.17.refs_4_
  93.1 1.2 %collective-permute-done.20.refs_7_ = bf16[4,32,128]{2,1,0:T(8,128)(2,1)S(1)} collective-permute-done((bf16[4,32,128]{2,1,0:T(8,128)(2,1)S(1)}, bf16[4,32,128]{2,1,0:T(8,128)(2,1)S(1)}, u32[]{:S(2)}, u32[]{:S(2)}) %collective-permute-start.20) | collective-permute-done | bytes 32800 | tf_op jit(solution)/shard_map/ppermute | solution.py:380
  94.3 6.3 %solve.1 = (f32[8,32,128]{2,1,0:T(8,128)}, f32[8,32,128]{2,1,0:T(8,128)}) custom-call(s32[1]{0:T(128)} %bitcast.side_ref.refs_0_, s32[1]{0:T(128)} %bitcast.1.refs_1_.me_ref, s32[4,8,128]{2,1,0:T(8,128)S(1)} %get-tuple-element.32.near_ref, f32[4,32,128]{2,1,0:T(8,128)S(1)} %get-tuple-element.37.refs_0_, ...), custom_call_target="tpu_custom_call" | custom-call | tf_op jit(solution)/shard_map/solve/pallas_call | solution.py:30
  (10 shorter events, 0.1 us)
Async XLA Ops:
  3.6 19.5 %collective-permute-start.2 = (bf16[592,128]{1,0:T(8,128)(2,1)S(1)}, bf16[592,128]{1,0:T(8,128)(2,1)S(1)}, u32[]{:S(2)}, u32[]{:S(2)}) collective-permute-start(bf16[592,128]{1,0:T(8,128)(2,1)S(1)} %get-tuple-element.21.refs_5_.refs_0_), channel_id=1, source_target_pairs={{0,12},{4,8},{8,4},{12,0},{1,13},{5,9},{9,5},{13,1},{2,14},{6,10},... | collective-permute-start | bytes 454664 | tf_op jit(solution)/shard_map/ppermute | solution.py:380
  8.7 30.1 %collective-permute-start.1 = (bf16[592,128]{1,0:T(8,128)(2,1)S(1)}, bf16[592,128]{1,0:T(8,128)(2,1)S(1)}, u32[]{:S(2)}, u32[]{:S(2)}) collective-permute-start(bf16[592,128]{1,0:T(8,128)(2,1)S(1)} %get-tuple-element.21.refs_5_.refs_0_), channel_id=1, source_target_pairs={{0,8},{4,12},{8,0},{12,4},{1,9},{5,13},{9,1},{13,5},{2,10},{6,14},... | collective-permute-start | bytes 454664 | tf_op jit(solution)/shard_map/ppermute | solution.py:380
  37.5 1.3 %collective-permute-start.6 = (f32[4,32,128]{2,1,0:T(8,128)S(1)}, f32[4,32,128]{2,1,0:T(8,128)S(1)}, u32[]{:S(2)}, u32[]{:S(2)}) collective-permute-start(f32[4,32,128]{2,1,0:T(8,128)S(1)} %get-tuple-element.26.refs_6_.refs_0_), channel_id=1, source_target_pairs={{0,1},{1,0},{2,3},{3,2},{4,5},{5,4},{6,7},{7,6},{8,9},{9,8},{10,11... | collective-permute-start | bytes 196616 | tf_op jit(solution)/shard_map/ppermute | solution.py:380
  37.6 16.7 %collective-permute-start = (bf16[592,128]{1,0:T(8,128)(2,1)S(1)}, bf16[592,128]{1,0:T(8,128)(2,1)S(1)}, u32[]{:S(2)}, u32[]{:S(2)}) collective-permute-start(bf16[592,128]{1,0:T(8,128)(2,1)S(1)} %get-tuple-element.21.refs_5_.refs_0_), channel_id=1, source_target_pairs={{0,4},{4,0},{8,12},{12,8},{1,5},{5,1},{9,13},{13,9},{2,6},{6,2},{1... | collective-permute-start | bytes 454664 | tf_op jit(solution)/shard_map/ppermute | solution.py:380
  53.2 1.3 %collective-permute-start.7 = (f32[4,32,128]{2,1,0:T(8,128)S(1)}, f32[4,32,128]{2,1,0:T(8,128)S(1)}, u32[]{:S(2)}, u32[]{:S(2)}) collective-permute-start(f32[4,32,128]{2,1,0:T(8,128)S(1)} %get-tuple-element.28.refs_6_.refs_0_), channel_id=1, source_target_pairs={{0,1},{1,0},{2,3},{3,2},{4,5},{5,4},{6,7},{7,6},{8,9},{9,8},{10,11... | collective-permute-start | bytes 196616 | tf_op jit(solution)/shard_map/ppermute | solution.py:380
  53.4 18.7 %collective-permute-start.9 = (f32[4,32,128]{2,1,0:T(8,128)S(1)}, f32[4,32,128]{2,1,0:T(8,128)S(1)}, u32[]{:S(2)}, u32[]{:S(2)}) collective-permute-start(f32[4,32,128]{2,1,0:T(8,128)S(1)} %get-tuple-element.25.refs_6_), channel_id=1, source_target_pairs={{0,1},{1,0},{2,3},{3,2},{4,5},{5,4},{6,7},{7,6},{8,9},{9,8},{10,11... | collective-permute-start | bytes 196616 | tf_op jit(solution)/shard_map/ppermute | solution.py:380
  53.8 20.0 %collective-permute-start.4 = (bf16[592,128]{1,0:T(8,128)(2,1)S(1)}, bf16[592,128]{1,0:T(8,128)(2,1)S(1)}, u32[]{:S(2)}, u32[]{:S(2)}) collective-permute-start(bf16[592,128]{1,0:T(8,128)(2,1)S(1)} %collective-permute-done.1.refs_5_.refs_2_), channel_id=1, source_target_pairs={{0,1},{1,0},{2,3},{3,2},{4,5},{5,4},{6,7},{7,6},{8,9},{9,8},{10,11... | collective-permute-start | bytes 454664 | tf_op jit(solution)/shard_map/ppermute | solution.py:380
  54.0 19.9 %collective-permute-start.5 = (bf16[592,128]{1,0:T(8,128)(2,1)S(1)}, bf16[592,128]{1,0:T(8,128)(2,1)S(1)}, u32[]{:S(2)}, u32[]{:S(2)}) collective-permute-start(bf16[592,128]{1,0:T(8,128)(2,1)S(1)} %collective-permute-done.2.refs_5_.refs_3_), channel_id=1, source_target_pairs={{0,1},{1,0},{2,3},{3,2},{4,5},{5,4},{6,7},{7,6},{8,9},{9,8},{10,11... | collective-permute-start | bytes 454664 | tf_op jit(solution)/shard_map/ppermute | solution.py:380
  54.3 19.5 %collective-permute-start.3 = (bf16[592,128]{1,0:T(8,128)(2,1)S(1)}, bf16[592,128]{1,0:T(8,128)(2,1)S(1)}, u32[]{:S(2)}, u32[]{:S(2)}) collective-permute-start(bf16[592,128]{1,0:T(8,128)(2,1)S(1)} %collective-permute-done.refs_5_.refs_1_), channel_id=1, source_target_pairs={{0,1},{1,0},{2,3},{3,2},{4,5},{5,4},{6,7},{7,6},{8,9},{9,8},{10,11... | collective-permute-start | bytes 454664 | tf_op jit(solution)/shard_map/ppermute | solution.py:380
  54.5 17.7 %collective-permute-start.10 = (f32[4,32,128]{2,1,0:T(8,128)S(1)}, f32[4,32,128]{2,1,0:T(8,128)S(1)}, u32[]{:S(2)}, u32[]{:S(2)}) collective-permute-start(f32[4,32,128]{2,1,0:T(8,128)S(1)} %add.7.refs_7_), channel_id=1, source_target_pairs={{0,12},{4,8},{8,4},{12,0},{1,13},{5,9},{9,5},{13,1},{2,14},{6,10},... | collective-permute-start | bytes 196616 | tf_op jit(solution)/shard_map/ppermute | solution.py:380
  72.2 1.3 %collective-permute-start.8 = (f32[4,32,128]{2,1,0:T(8,128)S(1)}, f32[4,32,128]{2,1,0:T(8,128)S(1)}, u32[]{:S(2)}, u32[]{:S(2)}) collective-permute-start(f32[4,32,128]{2,1,0:T(8,128)S(1)} %get-tuple-element.31.refs_0_), channel_id=1, source_target_pairs={{0,1},{1,0},{2,3},{3,2},{4,5},{5,4},{6,7},{7,6},{8,9},{9,8},{10,11... | collective-permute-start | bytes 196616 | tf_op jit(solution)/shard_map/ppermute | solution.py:380
  72.3 6.7 %collective-permute-start.11 = (f32[4,32,128]{2,1,0:T(8,128)S(1)}, f32[4,32,128]{2,1,0:T(8,128)S(1)}, u32[]{:S(2)}, u32[]{:S(2)}) collective-permute-start(f32[4,32,128]{2,1,0:T(8,128)S(1)} %add.8.refs_7_), channel_id=1, source_target_pairs={{0,8},{4,12},{8,0},{12,4},{1,9},{5,13},{9,1},{13,5},{2,10},{6,14},... | collective-permute-start | bytes 196616 | tf_op jit(solution)/shard_map/ppermute | solution.py:380
  73.5 5.7 %collective-permute-start.12 = (f32[4,32,128]{2,1,0:T(8,128)S(1)}, f32[4,32,128]{2,1,0:T(8,128)S(1)}, u32[]{:S(2)}, u32[]{:S(2)}) collective-permute-start(f32[4,32,128]{2,1,0:T(8,128)S(1)} %add.9.refs_7_), channel_id=1, source_target_pairs={{0,4},{4,0},{8,12},{12,8},{1,5},{5,1},{9,13},{13,9},{2,6},{6,2},{1... | collective-permute-start | bytes 196616 | tf_op jit(solution)/shard_map/ppermute | solution.py:380
  79.2 6.7 %collective-permute-start.13 = (f32[4,32,128]{2,1,0:T(8,128)S(1)}, f32[4,32,128]{2,1,0:T(8,128)S(1)}, u32[]{:S(2)}, u32[]{:S(2)}) collective-permute-start(f32[4,32,128]{2,1,0:T(8,128)S(1)} %add.13.refs_0_.x_ref), channel_id=1, source_target_pairs={{0,2},{2,0},{1,3},{3,1},{4,6},{6,4},{5,7},{7,5},{8,10},{10,8},{9,1... | collective-permute-start | bytes 196616 | tf_op jit(solution)/shard_map/ppermute | solution.py:380
  85.9 4.5 %collective-permute-start.14 = (bf16[4,32,128]{2,1,0:T(8,128)(2,1)S(1)}, bf16[4,32,128]{2,1,0:T(8,128)(2,1)S(1)}, u32[]{:S(2)}, u32[]{:S(2)}) collective-permute-start(bf16[4,32,128]{2,1,0:T(8,128)(2,1)S(1)} %get-tuple-element.38), channel_id=1, source_target_pairs={{0,4},{4,0},{8,12},{12,8},{1,5},{5,1},{9,13},{13,9},{2,6},{6,2},{1... | collective-permute-start | bytes 98312 | tf_op jit(solution)/shard_map/ppermute | solution.py:380
  85.9 4.9 %collective-permute-start.15 = (bf16[4,32,128]{2,1,0:T(8,128)(2,1)S(1)}, bf16[4,32,128]{2,1,0:T(8,128)(2,1)S(1)}, u32[]{:S(2)}, u32[]{:S(2)}) collective-permute-start(bf16[4,32,128]{2,1,0:T(8,128)(2,1)S(1)} %get-tuple-element.38), channel_id=1, source_target_pairs={{0,8},{4,12},{8,0},{12,4},{1,9},{5,13},{9,1},{13,5},{2,10},{6,14},... | collective-permute-start | bytes 98312 | tf_op jit(solution)/shard_map/ppermute | solution.py:380
  87.4 5.7 %collective-permute-start.17 = (f32[4,32,128]{2,1,0:T(8,128)S(1)}, f32[4,32,128]{2,1,0:T(8,128)S(1)}, u32[]{:S(2)}, u32[]{:S(2)}) collective-permute-start(f32[4,32,128]{2,1,0:T(8,128)S(1)} %get-tuple-element.37.refs_0_), channel_id=1, source_target_pairs={{0,1},{1,0},{2,3},{3,2},{4,5},{5,4},{6,7},{7,6},{8,9},{9,8},{10,11... | collective-permute-start | bytes 196616 | tf_op jit(solution)/shard_map/ppermute | solution.py:380
  87.4 5.7 %collective-permute-start.16 = (bf16[4,32,128]{2,1,0:T(8,128)(2,1)S(1)}, bf16[4,32,128]{2,1,0:T(8,128)(2,1)S(1)}, u32[]{:S(2)}, u32[]{:S(2)}) collective-permute-start(bf16[4,32,128]{2,1,0:T(8,128)(2,1)S(1)} %get-tuple-element.38), channel_id=1, source_target_pairs={{0,12},{4,8},{8,4},{12,0},{1,13},{5,9},{9,5},{13,1},{2,14},{6,10},... | collective-permute-start | bytes 98312 | tf_op jit(solution)/shard_map/ppermute | solution.py:380
  90.3 2.8 %collective-permute-start.18 = (bf16[4,32,128]{2,1,0:T(8,128)(2,1)S(1)}, bf16[4,32,128]{2,1,0:T(8,128)(2,1)S(1)}, u32[]{:S(2)}, u32[]{:S(2)}) collective-permute-start(bf16[4,32,128]{2,1,0:T(8,128)(2,1)S(1)} %collective-permute-done.14.refs_1_), channel_id=1, source_target_pairs={{0,1},{1,0},{2,3},{3,2},{4,5},{5,4},{6,7},{7,6},{8,9},{9,8},{10,11... | collective-permute-start | bytes 98312 | tf_op jit(solution)/shard_map/ppermute | solution.py:380
  90.8 2.3 %collective-permute-start.19 = (bf16[4,32,128]{2,1,0:T(8,128)(2,1)S(1)}, bf16[4,32,128]{2,1,0:T(8,128)(2,1)S(1)}, u32[]{:S(2)}, u32[]{:S(2)}) collective-permute-start(bf16[4,32,128]{2,1,0:T(8,128)(2,1)S(1)} %collective-permute-done.15.refs_2_), channel_id=1, source_target_pairs={{0,1},{1,0},{2,3},{3,2},{4,5},{5,4},{6,7},{7,6},{8,9},{9,8},{10,11... | collective-permute-start | bytes 98312 | tf_op jit(solution)/shard_map/ppermute | solution.py:380
  93.1 1.2 %collective-permute-start.20 = (bf16[4,32,128]{2,1,0:T(8,128)(2,1)S(1)}, bf16[4,32,128]{2,1,0:T(8,128)(2,1)S(1)}, u32[]{:S(2)}, u32[]{:S(2)}) collective-permute-start(bf16[4,32,128]{2,1,0:T(8,128)(2,1)S(1)} %collective-permute-done.16.refs_3_), channel_id=1, source_target_pairs={{0,1},{1,0},{2,3},{3,2},{4,5},{5,4},{6,7},{7,6},{8,9},{9,8},{10,11... | collective-permute-start | bytes 98312 | tf_op jit(solution)/shard_map/ppermute | solution.py:380
